TPU v7x, 32 devices: a whole 2x2x4 slice. The times are simulated.
32 devices in a mesh: groups: 2 (over y), feat: 8 (over z, core), tok: 2 (over x).
Axes of the slice: x: 2, y: 2, z: 4, core: 2. Of those that a mesh axis runs over, the one named last changes fastest.
Arguments:
- tokens: bfloat16 [1024, 4096], P(('groups', 'feat'), 'tok'), parts along dimension 0, may hold values from -6 to 6
- out_grad: bfloat16 [1024, 4096], P(('groups', 'feat'), 'tok'), parts along dimension 0, may hold values from -0.75 to 0.75
- gate_weight: bfloat16 [4096, 14336], P('tok', 'feat'), may hold values from -0.09375 to 0.09375
- up_weight: bfloat16 [4096, 14336], P('tok', 'feat'), may hold values from -0.09375 to 0.09375
- down_weight: bfloat16 [14336, 4096], P('feat', 'tok'), may hold values from -0.046875 to 0.046875
Outputs:
- grad_gate: bfloat16 [8192, 14336], P(('groups', 'tok'), 'feat'), parts along dimension 0
- grad_up: bfloat16 [8192, 14336], P(('groups', 'tok'), 'feat'), parts along dimension 0
- grad_down: bfloat16 [28672, 4096], P(('groups', 'feat'), 'tok'), parts along dimension 0
There are 2 independent parts, one for each index of `groups`. A program takes and returns all parts, laid end to end along the dimension named above; an argument that names none is the same for every part. Nothing has to cross between parts.
All inputs are finite; a program needn't handle non-finite values.
Results may differ from a plain program's by a relative error of at most 0.005.
Values may be sent and summed in bfloat16 or wider, within the bound.
A program may use at most 128 MiB of HBM per device.

v0:
```python
import jax
import jax.numpy as jnp
from jax import lax
from jax.sharding import PartitionSpec as P


def contract_rows(left, right):
    return lax.dot_general(
        left, right, (((0,), (0,)), ((), ())), preferred_element_type=jnp.float32
    )


def swiglu_parts(gate, up, grad_hidden):
    sigmoid_gate = jax.nn.sigmoid(gate)
    activated = gate * sigmoid_gate
    hidden = (activated * up).astype(jnp.bfloat16)
    gate_delta = (grad_hidden * up * sigmoid_gate * (1.0 + gate * (1.0 - sigmoid_gate))).astype(
        jnp.bfloat16
    )
    up_delta = (grad_hidden * activated).astype(jnp.bfloat16)
    return (hidden, gate_delta, up_delta)


def shards(tokens, out_grad, gate_weight, up_weight, down_weight):
    token_rows, grad_rows = (
        lax.all_gather(tokens, "feat", axis=0, tiled=True),
        lax.all_gather(out_grad, "feat", axis=0, tiled=True),
    )
    gate_part = jnp.dot(token_rows, gate_weight, preferred_element_type=jnp.float32)
    up_part = jnp.dot(token_rows, up_weight, preferred_element_type=jnp.float32)
    hidden_part = lax.dot_general(
        grad_rows, down_weight, (((1,), (1,)), ((), ())), preferred_element_type=jnp.float32
    )
    gate, up = (
        lax.psum_scatter(gate_part, "tok", scatter_dimension=0, tiled=True),
        lax.psum_scatter(up_part, "tok", scatter_dimension=0, tiled=True),
    )
    grad_hidden = lax.psum_scatter(hidden_part, "tok", scatter_dimension=0, tiled=True)
    hidden, gate_delta, up_delta = swiglu_parts(gate, up, grad_hidden)
    hidden, gate_delta, up_delta = (
        lax.all_gather(hidden, "tok", axis=0, tiled=True),
        lax.all_gather(gate_delta, "tok", axis=0, tiled=True),
        lax.all_gather(up_delta, "tok", axis=0, tiled=True),
    )
    grad_gate = contract_rows(token_rows, gate_delta).astype(jnp.bfloat16)
    grad_up = contract_rows(token_rows, up_delta).astype(jnp.bfloat16)
    grad_down = contract_rows(hidden, grad_rows).astype(jnp.bfloat16)
    return (grad_gate, grad_up, grad_down)


def solution(mesh):
    return jax.shard_map(
        shards,
        mesh=mesh,
        in_specs=(
            P(("groups", "feat"), "tok"),
            P(("groups", "feat"), "tok"),
            P("tok", "feat"),
            P("tok", "feat"),
            P("feat", "tok"),
        ),
        out_specs=(
            P(("groups", "tok"), "feat"),
            P(("groups", "tok"), "feat"),
            P(("groups", "feat"), "tok"),
        ),
        check_vma=False,
    )
```

profile of v0, /device:TPU:0, one launch (start us, length us, event | category | flops | bytes accessed | tf_op | source)
XLA Modules:
  0.0 340.8 jit_solution(12979034745607124488)
XLA Ops:
  7.2 0.7 all-gather.8.cloned.1.call-update
  7.9 0.7 all-gather.6.cloned.1.call-update
  8.7 32.7 %all-gather.8.cloned.1.call-done = bf16[512,2048]{1,0:T(8,128)(2,1)} async-done(((bf16[64,2048]{1,0:T(8,128)(2,1)}), bf16[512,2048]{1,0:T(8,128)(2,1)}) %all-gather.8.cloned.1.call-update) | async-done | bytes 2097168 | tf_op jit(solution)/shard_map/all_gather | solution.py:26
  41.4 9.5 %fusion.4 = f32[512,1792]{1,0:T(8,128)} fusion(bf16[512,2048]{1,0:T(8,128)(2,1)} %all-gather.8.cloned.1.call-done, bf16[2048,1792]{1,0:T(8,128)(2,1)} %param.8), kind=kOutput, calls=%fused_computation.11 | convolution fusion | flops 3758096384 | bytes 13107200 | tf_op jit(solution)/shard_map/dot_general | solution.py:30
  51.0 0.0 reduce-scatter.8.cloned.1.call-start
  51.0 1.5 copy-done.1
  52.5 8.9 %fusion.5 = f32[512,1792]{1,0:T(8,128)} fusion(bf16[512,2048]{1,0:T(8,128)(2,1)S(1)} %copy-done.1, bf16[2048,1792]{1,0:T(8,128)(2,1)} %param.7), kind=kOutput, calls=%fused_computation.12 | convolution fusion | flops 3758096384 | bytes 13107200 | tf_op jit(solution)/shard_map/dot_general | solution.py:29
  61.5 10.2 %all-gather.6.cloned.1.call-done = bf16[512,2048]{1,0:T(8,128)(2,1)} async-done(((bf16[64,2048]{1,0:T(8,128)(2,1)}), bf16[512,2048]{1,0:T(8,128)(2,1)}) %all-gather.6.cloned.1.call-update) | async-done | bytes 2097168 | tf_op jit(solution)/shard_map/all_gather | solution.py:27
  71.7 9.9 %fusion.3 = f32[512,1792]{1,0:T(8,128)} fusion(bf16[512,2048]{1,0:T(8,128)(2,1)} %all-gather.6.cloned.1.call-done, bf16[1792,2048]{1,0:T(8,128)(2,1)} %param.9), kind=kOutput, calls=%fused_computation.10 | convolution fusion | flops 3758096384 | bytes 13107200 | tf_op jit(solution)/shard_map/dot_general | solution.py:31
  81.6 41.5 %reduce-scatter.6.cloned.1.call-done = f32[256,1792]{1,0:T(8,128)} async-done(((f32[512,1792]{1,0:T(8,128)}), f32[256,1792]{1,0:T(8,128)}) %reduce-scatter.6.cloned.1.call-update) | async-done | bytes 1835024 | tf_op jit(solution)/shard_map/reduce_scatter | solution.py:36
  123.1 51.9 %reduce-scatter.8.cloned.1.call-done = f32[256,1792]{1,0:T(8,128)} async-done(((f32[512,1792]{1,0:T(8,128)}), f32[256,1792]{1,0:T(8,128)}) %reduce-scatter.8.cloned.1.call-update) | async-done | bytes 1835024 | tf_op jit(solution)/shard_map/reduce_scatter | solution.py:35
  175.0 51.8 %reduce-scatter.4.cloned.1.call-done = f32[256,1792]{1,0:T(8,128)} async-done(((f32[512,1792]{1,0:T(8,128)}), f32[256,1792]{1,0:T(8,128)}) %reduce-scatter.4.cloned.1.call-update) | async-done | bytes 1835024 | tf_op jit(solution)/shard_map/reduce_scatter | solution.py:38
  226.8 5.0 %multiply_convert_fusion = (bf16[256,1792]{1,0:T(8,128)(2,1)}, bf16[256,1792]{1,0:T(8,128)(2,1)}, bf16[256,1792]{1,0:T(8,128)(2,1)}) fusion(f32[256,1792]{1,0:T(8,128)} %reduce-scatter.6.cloned.1.call-done, f32[256,1792]{1,0:T(8,128)} %reduce-scatter.8.cloned.1.call-done, f32[256,1792]{1,0:T(8,128)} %reduce-scatter.4.cloned.1.call-done), kind=kLoop, calls=%fused_computation.5 | loop fusion | flops 6881280 | bytes 8257536 | tf_op jit(solution)/shard_map/convert_element_type | solution.py:16
  231.9 0.7 all-gather.10.cloned.1.call-update
  232.6 0.2 all-gather.14.cloned.1.call-start
  232.9 0.5 all-gather.14.cloned.1.call-update
  233.4 28.8 %all-gather.12.cloned.1.call-done = bf16[512,1792]{1,0:T(8,128)(2,1)} async-done(((bf16[256,1792]{1,0:T(8,128)(2,1)}), bf16[512,1792]{1,0:T(8,128)(2,1)}) %all-gather.12.cloned.1.call-update) | async-done | bytes 1835024 | tf_op jit(solution)/shard_map/all_gather | solution.py:43
  262.2 7.5 %fusion.1 = bf16[2048,1792]{0,1:T(8,128)(2,1)} fusion(bf16[512,1792]{1,0:T(8,128)(2,1)} %all-gather.12.cloned.1.call-done, bf16[512,2048]{1,0:T(8,128)(2,1)S(1)} %copy-done.1), kind=kOutput, calls=%fused_computation.4 | convolution fusion | flops 3761766400 | bytes 11272192 | tf_op jit(solution)/shard_map/dot_general | solution.py:8
  269.8 10.0 %copy.9 = bf16[2048,1792]{1,0:T(8,128)(2,1)} copy(bf16[2048,1792]{0,1:T(8,128)(2,1)} %fusion.1) | data formatting | bytes 14680064
  279.8 14.8 %all-gather.10.cloned.1.call-done = bf16[512,1792]{1,0:T(8,128)(2,1)} async-done(((bf16[256,1792]{1,0:T(8,128)(2,1)}), bf16[512,1792]{1,0:T(8,128)(2,1)}) %all-gather.10.cloned.1.call-update) | async-done | bytes 1835024 | tf_op jit(solution)/shard_map/all_gather | solution.py:42
  294.6 7.6 %fusion = bf16[2048,1792]{0,1:T(8,128)(2,1)} fusion(bf16[512,1792]{1,0:T(8,128)(2,1)} %all-gather.10.cloned.1.call-done, bf16[512,2048]{1,0:T(8,128)(2,1)S(1)} %copy-done.1), kind=kOutput, calls=%fused_computation.3 | convolution fusion | flops 3761766400 | bytes 11272192 | tf_op jit(solution)/shard_map/dot_general | solution.py:8
  302.2 10.2 %copy.8 = bf16[2048,1792]{1,0:T(8,128)(2,1)} copy(bf16[2048,1792]{0,1:T(8,128)(2,1)} %fusion) | data formatting | bytes 14680064
  312.3 14.1 %all-gather.14.cloned.1.call-done = bf16[512,1792]{1,0:T(8,128)(2,1)} async-done(((bf16[256,1792]{1,0:T(8,128)(2,1)}), bf16[512,1792]{1,0:T(8,128)(2,1)}) %all-gather.14.cloned.1.call-update) | async-done | bytes 1835024 | tf_op jit(solution)/shard_map/all_gather | solution.py:41
  326.4 7.6 %convolution_convert_fusion = bf16[1792,2048]{1,0:T(8,128)(2,1)} fusion(bf16[512,1792]{1,0:T(8,128)(2,1)} %all-gather.14.cloned.1.call-done, bf16[512,2048]{1,0:T(8,128)(2,1)S(1)} %copy-done), kind=kOutput, calls=%fused_computation | convolution fusion | flops 3761766400 | bytes 11272192 | tf_op jit(solution)/shard_map/dot_general | solution.py:8
  (13 shorter events, 0.3 us)
Async XLA Ops:
  7.2 34.3 %all-gather.8.cloned.1.call-start = ((), (), s32[]{:S(2)}) async-start(), calls=%async_computation.5 | async-start | bytes 2359296 | tf_op jit(solution)/shard_map/all_gather | solution.py:26
  7.9 63.8 %all-gather.6.cloned.1.call-start = ((), (), s32[]{:S(2)}) async-start(), calls=%async_computation.3 | async-start | bytes 2359296 | tf_op jit(solution)/shard_map/all_gather | solution.py:27
  8.6 114.5 %reduce-scatter.6.cloned.1.call-start = ((), (), s32[]{:S(2)}) async-start(), calls=%async_computation.6 | async-start | bytes 5505024 | tf_op jit(solution)/shard_map/reduce_scatter | solution.py:36
  50.9 1.6 copy-start.1
  51.0 124.1 %reduce-scatter.8.cloned.1.call-start = ((), (), s32[]{:S(2)}) async-start(), calls=%async_computation.7 | async-start | bytes 5505024 | tf_op jit(solution)/shard_map/reduce_scatter | solution.py:35
  61.4 165.4 %reduce-scatter.4.cloned.1.call-start = ((), (), s32[]{:S(2)}) async-start(), calls=%async_computation.4 | async-start | bytes 5505024 | tf_op jit(solution)/shard_map/reduce_scatter | solution.py:38
  81.6 180.6 %all-gather.12.cloned.1.call-start = ((), (), s32[]{:S(2)}) async-start(), calls=%async_computation.9 | async-start | bytes 2752512 | tf_op jit(solution)/shard_map/all_gather | solution.py:43
  231.9 62.7 %all-gather.10.cloned.1.call-start = ((), (), s32[]{:S(2)}) async-start(), calls=%async_computation.8 | async-start | bytes 2752512 | tf_op jit(solution)/shard_map/all_gather | solution.py:42
  232.6 93.8 %all-gather.14.cloned.1.call-start = ((), (), s32[]{:S(2)}) async-start(), calls=%async_computation.10 | async-start | bytes 2752512 | tf_op jit(solution)/shard_map/all_gather | solution.py:41
  302.2 24.3 %copy-start = (bf16[512,2048]{1,0:T(8,128)(2,1)S(1)}, bf16[512,2048]{1,0:T(8,128)(2,1)}, u32[]{:S(2)}) copy-start(bf16[512,2048]{1,0:T(8,128)(2,1)} %all-gather.6.cloned.1.call-done) | copy-start | bytes 6291460
Sparse Core Ops, SparseCore 0:
  9.6 31.7 all-gather.7
  43.0 28.5 all-gather.5
  74.5 48.5 reduce-scatter.5
  125.9 49.0 reduce-scatter.7
  177.7 49.0 reduce-scatter.3
  232.0 30.1 all-gather.11
  264.4 30.1 all-gather.9
  296.2 30.1 all-gather.13
where the time goes:
time: 342 us; the launch traced here: 341 us
  waiting for transfers between devices  248 us (73%)
  matrix products  50.9 us (15%)
  local copies, waits for them, and re-layouts  21.7 us (6%)
  between operations  14.1 us (4%)
  other arithmetic  5.03 us (1%)
    reduce_scatter x1, waiting for transfers between devices, shards(): lax.psum_scatter(gate_part, 'tok', scatter_dimension=0, tiled=True)  51.9 us
    reduce_scatter x1, waiting for transfers between devices, shards(): lax.psum_scatter(hidden_part, 'tok', scatter_dimension=0, tiled=True)  51.8 us
    reduce_scatter x1, waiting for transfers between devices, shards(): lax.psum_scatter(up_part, 'tok', scatter_dimension=0, tiled=True)  41.5 us
    all_gather x1, waiting for transfers between devices, shards(): lax.all_gather(tokens, 'feat', axis=0, tiled=True)  32.7 us
    all_gather x1, waiting for transfers between devices, shards(): lax.all_gather(up_delta, 'tok', axis=0, tiled=True)  28.8 us
    dot_general x3, matrix products, contract_rows(): lax.dot_general(left, right, (((0,), (0,)), ((), ())), preferred_element_...  22.7 us
    unnamed x6, local copies, waits for them, and re-layouts  21.7 us
    all_gather x1, waiting for transfers between devices, shards(): lax.all_gather(gate_delta, 'tok', axis=0, tiled=True)  14.8 us
  transfers between devices with their start and end apart: 8, of which 8 were waited for; matrix products, arithmetic and copies ran while one was open for 19% of the time, Pallas kernels for 0%

commit v1 on v0

--- a/solution.py
+++ b/solution.py
@@ -1,7 +1,15 @@
+import functools
+
 import jax
 import jax.numpy as jnp
 from jax import lax
+from jax.experimental import pallas as pl
+from jax.experimental.pallas import tpu as pltpu
 from jax.sharding import PartitionSpec as P
+
+CHUNK = 256
+VMEM_LIMIT = 48 * 1024 * 1024
+F32, BF16 = jnp.float32, jnp.bfloat16
 
 
 def contract_rows(left, right):
@@ -21,7 +29,7 @@
     return (hidden, gate_delta, up_delta)
 
 
-def shards(tokens, out_grad, gate_weight, up_weight, down_weight):
+def plain_shards(tokens, out_grad, gate_weight, up_weight, down_weight):
     token_rows, grad_rows = (
         lax.all_gather(tokens, "feat", axis=0, tiled=True),
         lax.all_gather(out_grad, "feat", axis=0, tiled=True),
@@ -31,16 +39,13 @@
     hidden_part = lax.dot_general(
         grad_rows, down_weight, (((1,), (1,)), ((), ())), preferred_element_type=jnp.float32
     )
-    gate, up = (
-        lax.psum_scatter(gate_part, "tok", scatter_dimension=0, tiled=True),
-        lax.psum_scatter(up_part, "tok", scatter_dimension=0, tiled=True),
-    )
-    grad_hidden = lax.psum_scatter(hidden_part, "tok", scatter_dimension=0, tiled=True)
-    hidden, gate_delta, up_delta = swiglu_parts(gate, up, grad_hidden)
+    gate, up, grad_hidden = (
+        lax.psum_scatter(part, "tok", scatter_dimension=0, tiled=True)
+        for part in (gate_part, up_part, hidden_part)
+    )
     hidden, gate_delta, up_delta = (
-        lax.all_gather(hidden, "tok", axis=0, tiled=True),
-        lax.all_gather(gate_delta, "tok", axis=0, tiled=True),
-        lax.all_gather(up_delta, "tok", axis=0, tiled=True),
+        lax.all_gather(part, "tok", axis=0, tiled=True)
+        for part in swiglu_parts(gate, up, grad_hidden)
     )
     grad_gate = contract_rows(token_rows, gate_delta).astype(jnp.bfloat16)
     grad_up = contract_rows(token_rows, up_delta).astype(jnp.bfloat16)
@@ -48,9 +53,259 @@
     return (grad_gate, grad_up, grad_down)
 
 
+def partial_kernel(n_token, n_grad, *refs):
+    refs = list(refs)
+    x_ref = refs.pop(0) if n_token else None
+    w_refs = [refs.pop(0) for _ in range(n_token)]
+    g_ref = refs.pop(0) if n_grad else None
+    d_refs = [refs.pop(0) for _ in range(n_grad)]
+    own_ref, send_ref = refs[-2:]
+    for i, w_ref in enumerate(w_refs):
+        part = jnp.dot(x_ref[...], w_ref[...], preferred_element_type=F32)
+        own_ref[i] = part
+        send_ref[i] = part.astype(BF16)
+    for i, d_ref in enumerate(d_refs):
+        part = lax.dot_general(
+            g_ref[...], d_ref[...], (((1,), (1,)), ((), ())), preferred_element_type=F32
+        )
+        own_ref[n_token + i] = part
+        send_ref[n_token + i] = part.astype(BF16)
+
+
+def partial_products(rows, grad_rows, n_rows, weights, down, first, count, after):
+    n_token, n_grad = len(weights), 0 if down is None else 1
+    any_rows = rows if n_token else grad_rows
+    depth = any_rows.shape[1]
+    args, specs = [], []
+    if n_token:
+        args.append(rows)
+        specs.append(pl.BlockSpec((n_rows, depth), lambda i: (0, 0)))
+        for w in weights:
+            args.append(w)
+            specs.append(pl.BlockSpec((depth, CHUNK), lambda i: (0, first + i)))
+    if n_grad:
+        args.append(grad_rows)
+        specs.append(pl.BlockSpec((n_rows, depth), lambda i: (0, 0)))
+        args.append(down)
+        specs.append(pl.BlockSpec((CHUNK, depth), lambda i: (first + i, 0)))
+    for a in after:
+        args.append(a)
+        specs.append(pl.BlockSpec(memory_space=pl.ANY))
+    n = n_token + n_grad
+    block = pl.BlockSpec((n, n_rows, CHUNK), lambda i: (0, 0, i))
+    shape = (n, n_rows, count * CHUNK)
+    return pl.pallas_call(
+        functools.partial(partial_kernel, n_token, n_grad),
+        grid=(count,),
+        in_specs=specs,
+        out_specs=[block, block],
+        out_shape=[jax.ShapeDtypeStruct(shape, F32), jax.ShapeDtypeStruct(shape, BF16)],
+        compiler_params=pltpu.CompilerParams(vmem_limit_bytes=VMEM_LIMIT),
+        cost_estimate=pl.CostEstimate(
+            flops=2 * n * n_rows * depth * count * CHUNK,
+            bytes_accessed=n * count * CHUNK * (2 * depth + 6 * n_rows) + 2 * n_rows * depth,
+            transcendentals=0,
+        ),
+    )(*args)
+
+
+def join_kernel(*refs):
+    out_ref, base = refs[-1], 0
+    for ref in refs[:-1]:
+        n = ref.shape[0]
+        out_ref[base : base + n, :] = ref[...]
+        base += n
+
+
+def join(pieces):
+    n_rows = sum(p.shape[0] for p in pieces)
+    depth = pieces[0].shape[1]
+    tile = depth // 4
+    return pl.pallas_call(
+        join_kernel,
+        grid=(4,),
+        in_specs=[pl.BlockSpec((p.shape[0], tile), lambda i: (0, i)) for p in pieces],
+        out_specs=pl.BlockSpec((n_rows, tile), lambda i: (0, i)),
+        out_shape=jax.ShapeDtypeStruct((n_rows, depth), BF16),
+        cost_estimate=pl.CostEstimate(
+            flops=0, bytes_accessed=4 * n_rows * depth, transcendentals=0
+        ),
+    )(*pieces)
+
+
+def flip_kernel(x_ref, *refs):
+    refs[-1][...] = x_ref[...].T
+
+
+def flip(x, after):
+    n_rows, depth = x.shape
+    tile = depth // 4
+    return pl.pallas_call(
+        flip_kernel,
+        grid=(4,),
+        in_specs=[pl.BlockSpec((n_rows, tile), lambda i: (0, i))]
+        + [pl.BlockSpec(memory_space=pl.ANY)] * len(after),
+        out_specs=pl.BlockSpec((tile, n_rows), lambda i: (i, 0)),
+        out_shape=jax.ShapeDtypeStruct((depth, n_rows), BF16),
+        cost_estimate=pl.CostEstimate(
+            flops=0, bytes_accessed=4 * n_rows * depth, transcendentals=0
+        ),
+    )(x, *after)
+
+
+def grads_kernel(
+    own_a, got_a, own_b, got_b, own_t, got_t, own_g, got_g, flipped, grads, *rest
+):
+    gg_ref, gu_ref, gd_ref, hidden_t, gate_delta, up_delta = rest[-6:]
+
+    @pl.when(pl.program_id(0) == 0)
+    def _():
+        base = 0
+        for gate, up, grad_hidden in (
+            (
+                own_t[0] + got_t[0].astype(F32),
+                own_t[1] + got_t[1].astype(F32),
+                own_g[0] + got_g[0].astype(F32),
+            ),
+            tuple(own_a[i] + got_a[i].astype(F32) for i in range(3)),
+            tuple(own_b[i] + got_b[i].astype(F32) for i in range(3)),
+        ):
+            sigmoid_gate = jax.nn.sigmoid(gate)
+            activated = gate * sigmoid_gate
+            n = gate.shape[0]
+            hidden_t[:, base : base + n] = (activated * up).T.astype(BF16)
+            gate_delta[base : base + n, :] = (
+                grad_hidden * up * sigmoid_gate * (1.0 + gate * (1.0 - sigmoid_gate))
+            ).astype(BF16)
+            up_delta[base : base + n, :] = (grad_hidden * activated).astype(BF16)
+            base += n
+
+    gg_ref[...] = jnp.dot(flipped[...], gate_delta[...], preferred_element_type=F32).astype(BF16)
+    gu_ref[...] = jnp.dot(flipped[...], up_delta[...], preferred_element_type=F32).astype(BF16)
+    gd_ref[...] = jnp.dot(hidden_t[...], grads[...], preferred_element_type=F32).astype(BF16)
+
+
+def chunk_grads(j, a, ja, b, jb, t, g, flipped, grads, hidden_units, so_far, after):
+    depth, n_tokens = flipped.shape
+    steps = 4
+    tile = depth // steps
+
+    def part(arr, k):
+        return pl.BlockSpec((arr.shape[0], arr.shape[1], CHUNK), lambda i: (0, 0, k))
+
+    args = [a[0], a[1], b[0], b[1], t[0], t[1], g[0], g[1], flipped, grads]
+    specs = [part(a[0], ja), part(a[1], ja), part(b[0], jb), part(b[1], jb)]
+    specs += [part(t[0], 0), part(t[1], 0), part(g[0], 0), part(g[1], 0)]
+    specs += [
+        pl.BlockSpec((tile, n_tokens), lambda i: (i, 0)),
+        pl.BlockSpec((n_tokens, tile), lambda i: (0, i)),
+    ]
+    aliases = {}
+    if so_far is not None:
+        for k, arr in enumerate(so_far):
+            aliases[len(args)] = k
+            args.append(arr)
+            specs.append(pl.BlockSpec(memory_space=pl.ANY))
+    for arr in after:
+        args.append(arr)
+        specs.append(pl.BlockSpec(memory_space=pl.ANY))
+    up_shape = jax.ShapeDtypeStruct((depth, hidden_units), BF16)
+    down_shape = jax.ShapeDtypeStruct((hidden_units, depth), BF16)
+    return pl.pallas_call(
+        grads_kernel,
+        grid=(steps,),
+        in_specs=specs,
+        out_specs=[
+            pl.BlockSpec((tile, CHUNK), lambda i: (i, j)),
+            pl.BlockSpec((tile, CHUNK), lambda i: (i, j)),
+            pl.BlockSpec((CHUNK, tile), lambda i: (j, i)),
+        ],
+        out_shape=[up_shape, up_shape, down_shape],
+        scratch_shapes=[
+            pltpu.VMEM((CHUNK, n_tokens), BF16),
+            pltpu.VMEM((n_tokens, CHUNK), BF16),
+            pltpu.VMEM((n_tokens, CHUNK), BF16),
+        ],
+        input_output_aliases=aliases,
+        compiler_params=pltpu.CompilerParams(vmem_limit_bytes=VMEM_LIMIT),
+        cost_estimate=pl.CostEstimate(
+            flops=6 * n_tokens * depth * CHUNK,
+            bytes_accessed=4 * n_tokens * depth + 18 * n_tokens * CHUNK + 6 * depth * CHUNK,
+            transcendentals=n_tokens * CHUNK,
+        ),
+    )(*args)
+
+
+def pair_shards(n_feat, tokens, out_grad, gate_weight, up_weight, down_weight):
+    hidden_units = gate_weight.shape[1]
+    n_chunks = hidden_units // CHUNK
+    weights = (gate_weight, up_weight)
+
+    def swap(x):
+        return lax.ppermute(x, "tok", [(0, 1), (1, 0)])
+
+    def sibling(x):
+        return lax.ppermute(x, "feat", [(i, i ^ 1) for i in range(n_feat)])
+
+    def gather(x):
+        got = [
+            lax.ppermute(x, "feat", [(i, (i + k) % n_feat) for i in range(n_feat)])
+            for k in range(2, n_feat, 2)
+        ]
+        return got + [sibling(piece) for piece in got]
+
+    lead = 2
+    n_own = tokens.shape[0]
+    partial = partial_products
+    own1, send1 = partial(tokens, out_grad, n_own, weights, down_weight, 0, lead, ())
+    got1 = swap(send1)
+    sib_tokens, sib_grad = sibling(tokens), sibling(out_grad)
+    all_tokens = join(gather(tokens) + [tokens, sib_tokens])
+    all_grad = join(gather(out_grad) + [out_grad, sib_grad])
+    n_rest = all_tokens.shape[0] - 2 * n_own
+    own2, send2 = partial(
+        tokens, out_grad, n_own, weights, down_weight, lead, n_chunks - lead, (own1,)
+    )
+    got2 = swap(send2)
+    own3, send3 = partial(
+        sib_tokens, sib_grad, n_own, weights, down_weight, 0, n_chunks, (own2, got1)
+    )
+    got3 = swap(send3)
+
+    t_parts, g_parts = [], []
+    order = [("t", 0), ("t", 1), ("g", 0), ("g", 1)]
+    for j in range(2, n_chunks):
+        order += [("t", j), ("g", j)]
+    gots = [got1, got2, got3]
+    last = own3
+    for kind, j in order:
+        after = (last, gots[-3])
+        if kind == "t":
+            own, send = partial(all_tokens, None, n_rest, weights, None, j, 1, after)
+        else:
+            own, send = partial(None, all_grad, n_rest, (), down_weight, j, 1, after)
+        last = own
+        got = swap(send)
+        gots.append(got)
+        (t_parts if kind == "t" else g_parts).append((own, got))
+
+    flipped = flip(all_tokens, (t_parts[1][0],))
+    outs = None
+    for j in range(n_chunks):
+        a, ja = ((own1, got1), j) if j < lead else ((own2, got2), j - lead)
+        after = (g_parts[j + 2][0],) if j + 2 < n_chunks else ()
+        outs = chunk_grads(
+            j, a, ja, (own3, got3), j, t_parts[j], g_parts[j], flipped, all_grad,
+            hidden_units, outs, after,
+        )
+    return tuple(outs)
+
+
 def solution(mesh):
+    n_feat, n_tok = mesh.shape["feat"], mesh.shape["tok"]
+    pair = n_tok == 2 and n_feat % 2 == 0 and 2 < n_feat <= 8
     return jax.shard_map(
-        shards,
+        functools.partial(pair_shards, n_feat) if pair else plain_shards,
         mesh=mesh,
         in_specs=(
             P(("groups", "feat"), "tok"),

time: 342 us -> 174 us (0.51)
  waiting for transfers between devices: 248 us -> 17.6 us
  Pallas kernels: 0 us -> 113 us
  matrix products: 50.9 us -> 0 us
  starting transfers between devices: 0.5 us -> 30.2 us
  between operations: 14.1 us -> 1.01 us
  local copies, waits for them, and re-layouts: 21.7 us -> 10.4 us
  other arithmetic: 5.03 us -> 0 us
    reduce_scatter x3 -> x0, waiting for transfers between devices: 145 us -> none  [the longest x1 51.9 us: shards(): lax.psum_scatter(gate_part, 'tok', scatter_dimension=0, tiled=True)]
    pallas_call x0 -> x27, Pallas kernels: none -> 113 us  [the longest x17 61 us: partial_products(): pl.pallas_call(functools.partial(partial_kernel, n_token, n_grad), grid=(...]
    all_gather x5 -> x0, waiting for transfers between devices: 101 us -> none  [the longest x1 32.7 us: shards(): lax.all_gather(tokens, 'feat', axis=0, tiled=True)]
    dot_general x6 -> x0, matrix products: 50.9 us -> none  [the longest x3 22.7 us: contract_rows(): lax.dot_general(left, right, (((0,), (0,)), ((), ())), preferred_element_...]
    ppermute x0 -> x31, starting transfers between devices: none -> 30.2 us  [the longest x17 20.2 us: swap(): return lax.ppermute(x, 'tok', [(0, 1), (1, 0)])]
    ppermute x0 -> x31, waiting for transfers between devices: none -> 17.6 us  [the longest x6 11.4 us: gather(): lax.ppermute(x, 'feat', [(i, (i + k) % n_feat) for i in range(n_feat)])]
    unnamed x6 -> x86, local copies, waits for them, and re-layouts: 21.7 us -> 10.4 us
    convert_element_type x1 -> x0, other arithmetic: 5.03 us -> none  [swiglu_parts(): hidden = (activated * up).astype(jnp.bfloat16)]
  transfers between devices with their start and end apart: 8 -> 31, of which waited for: 8 -> 5; matrix products, arithmetic and copies ran while one was open for 19% -> 0% of each run, Pallas kernels for 0% -> 60%
where the time goes in v1:
time: 174 us; the launch traced here: 172 us
  Pallas kernels  113 us (65%)
  starting transfers between devices  30.2 us (17%)
  waiting for transfers between devices  17.6 us (10%)
  local copies, waits for them, and re-layouts  10.4 us (6%)
    pallas_call x17, Pallas kernels, partial_products(): pl.pallas_call(functools.partial(partial_kernel, n_token, n_grad), grid=(...  61 us
    pallas_call x7, Pallas kernels, chunk_grads(): pl.pallas_call(grads_kernel, grid=(steps,), in_specs=specs, out_specs=[pl...  40.2 us
    ppermute x17, starting transfers between devices, swap(): return lax.ppermute(x, 'tok', [(0, 1), (1, 0)])  20.2 us
    ppermute x6, waiting for transfers between devices, gather(): lax.ppermute(x, 'feat', [(i, (i + k) % n_feat) for i in range(n_feat)])  11.4 us
    unnamed x86, local copies, waits for them, and re-layouts  10.4 us
    ppermute x6, starting transfers between devices, gather(): lax.ppermute(x, 'feat', [(i, (i + k) % n_feat) for i in range(n_feat)])  8.26 us
    pallas_call x2, Pallas kernels, join(): pl.pallas_call(join_kernel, grid=(4,), in_specs=[pl.BlockSpec((p.shape[0]...  7.52 us
    ppermute x17, waiting for transfers between devices, swap(): return lax.ppermute(x, 'tok', [(0, 1), (1, 0)])  4.46 us
  transfers between devices with their start and end apart: 31, of which 5 were waited for; matrix products, arithmetic and copies ran while one was open for 0% of the time, Pallas kernels for 60%

profile of v1, /device:TPU:0, one launch (start us, length us, event | category | flops | bytes accessed | tf_op | source)
XLA Modules:
  0.0 172.0 jit_solution(10992372198656376683)
XLA Ops:
  1.6 4.0 %shard_map.76 = (f32[3,64,512]{2,1,0:T(8,128)S(1)}, bf16[3,64,512]{2,1,0:T(8,128)(2,1)S(1)}) custom-call(bf16[64,2048]{1,0:T(8,128)(2,1)S(1)} %copy-done.27, bf16[2048,1792]{1,0:T(8,128)(2,1)} %refs_1_.32, bf16[2048,1792]{1,0:T(8,128)(2,1)} %refs_2_.19, bf16[64,2048]{1,0:T(8,128)(2,1)} %refs_6_.3, bf16[1792,2048]{1,0:T(8,128)(2,1)} %refs_1_.33), custom_call_target="tpu_custom_call" | custom-call | flops 402653184 | bytes 7143424 | tf_op jit(solution)/shard_map/pallas_call | solution.py:97
  5.6 3.0 %collective-permute-start.3 = (bf16[3,64,512]{2,1,0:T(8,128)(2,1)S(1)}, bf16[3,64,512]{2,1,0:T(8,128)(2,1)S(1)}, u32[]{:S(2)}, u32[]{:S(2)}) collective-permute-start(bf16[3,64,512]{2,1,0:T(8,128)(2,1)S(1)} %get-tuple-element.58), channel_id=1, source_target_pairs={{0,1},{1,0},{2,3},{3,2},{4,5},{5,4},{6,7},{7,6},{8,9},{9,8},{10,11... | collective-permute-start | bytes 589832 | tf_op jit(solution)/shard_map/ppermute | solution.py:245
  9.1 3.6 %collective-permute-start.7 = (bf16[64,2048]{1,0:T(8,128)(2,1)S(1)}, bf16[64,2048]{1,0:T(8,128)(2,1)S(1)}, u32[]{:S(2)}, u32[]{:S(2)}) collective-permute-start(bf16[64,2048]{1,0:T(8,128)(2,1)S(1)} %copy-done.27), channel_id=1, source_target_pairs={{0,12},{2,14},{4,0},{6,2},{8,4},{10,6},{12,8},{14,10},{1,13},{3,15... | collective-permute-start | bytes 786440 | tf_op jit(solution)/shard_map/ppermute | solution.py:252
  13.5 2.8 %collective-permute-start.6 = (bf16[64,2048]{1,0:T(8,128)(2,1)S(1)}, bf16[64,2048]{1,0:T(8,128)(2,1)S(1)}, u32[]{:S(2)}, u32[]{:S(2)}) collective-permute-start(bf16[64,2048]{1,0:T(8,128)(2,1)S(1)} %copy-done.27), channel_id=1, source_target_pairs={{0,8},{2,10},{4,12},{6,14},{8,0},{10,2},{12,4},{14,6},{1,9},{3,11}... | collective-permute-start | bytes 786440 | tf_op jit(solution)/shard_map/ppermute | solution.py:252
  17.9 9.4 %shard_map.77 = (f32[3,64,1280]{2,1,0:T(8,128)S(1)}, bf16[3,64,1280]{2,1,0:T(8,128)(2,1)}) custom-call(bf16[64,2048]{1,0:T(8,128)(2,1)S(1)} %copy-done.27, bf16[2048,1792]{1,0:T(8,128)(2,1)} %refs_1_.32, bf16[2048,1792]{1,0:T(8,128)(2,1)} %refs_2_.19, bf16[64,2048]{1,0:T(8,128)(2,1)} %refs_6_.3, bf16[1792,2048]{1,0:T(8,128)(2,1)} %refs_1_.33, ...), custom_call_target="tpu_custom_call" | custom-call | flops 1006632960 | bytes 17465344 | tf_op jit(solution)/shard_map/pallas_call | solution.py:97
  29.4 11.4 %collective-permute-done.6.refs_1_ = bf16[64,2048]{1,0:T(8,128)(2,1)S(1)} collective-permute-done((bf16[64,2048]{1,0:T(8,128)(2,1)S(1)}, bf16[64,2048]{1,0:T(8,128)(2,1)S(1)}, u32[]{:S(2)}, u32[]{:S(2)}) %collective-permute-start.6) | collective-permute-done | bytes 262176 | tf_op jit(solution)/shard_map/ppermute | solution.py:252
  40.8 12.0 %shard_map.78 = (f32[3,64,1792]{2,1,0:T(8,128)S(1)}, bf16[3,64,1792]{2,1,0:T(8,128)(2,1)}) custom-call(bf16[64,2048]{1,0:T(8,128)(2,1)S(1)} %collective-permute-done.1.refs_0_.refs_7_, bf16[2048,1792]{1,0:T(8,128)(2,1)} %refs_1_.32, bf16[2048,1792]{1,0:T(8,128)(2,1)} %refs_2_.19, bf16[64,2048]{1,0:T(8,128)(2,1)S(1)} %collective-permute-done.2.refs_3_.refs_7_, ...), custom_call_target="tpu_custom_call" | custom-call | flops 1409286144 | bytes 24346624 | tf_op jit(solution)/shard_map/pallas_call | solution.py:97
  55.1 3.7 %shard_map.79.refs_0_.x_ref = bf16[512,2048]{1,0:T(8,128)(2,1)} custom-call(bf16[64,2048]{1,0:T(8,128)(2,1)} %copy-done.38, bf16[64,2048]{1,0:T(8,128)(2,1)} %copy-done.39, bf16[64,2048]{1,0:T(8,128)(2,1)} %copy-done.37, bf16[64,2048]{1,0:T(8,128)(2,1)} %copy-done.41, bf16[64,2048]{1,0:T(8,128)(2,1)} %copy-done.42, bf16[64,2048]{1,0:T(8,128)(2,1)} %copy-done.40, ...), custom_call_target="tpu_custom_call" | custom-call | bytes 4194304 | tf_op jit(solution)/shard_map/pallas_call | solution.py:124
  60.4 3.4 %shard_map.81 = (f32[2,384,256]{2,1,0:T(8,128)S(1)}, bf16[2,384,256]{2,1,0:T(8,128)(2,1)}) custom-call(bf16[512,2048]{1,0:T(8,128)(2,1)S(1)} %copy-done.6, bf16[2048,1792]{1,0:T(8,128)(2,1)} %refs_1_.32, bf16[2048,1792]{1,0:T(8,128)(2,1)} %refs_2_.19, f32[3,64,1792]{2,1,0:T(8,128)S(1)} %get-tuple-element.59.refs_3_.own_b, ...), custom_call_target="tpu_custom_call" | custom-call | flops 805306368 | bytes 4849664 | tf_op jit(solution)/shard_map/pallas_call | solution.py:97
  65.4 3.3 %shard_map.82 = (f32[2,384,256]{2,1,0:T(8,128)S(1)}, bf16[2,384,256]{2,1,0:T(8,128)(2,1)}) custom-call(bf16[512,2048]{1,0:T(8,128)(2,1)S(1)} %copy-done.7, bf16[2048,1792]{1,0:T(8,128)(2,1)} %refs_1_.32, bf16[2048,1792]{1,0:T(8,128)(2,1)} %refs_2_.19, f32[2,384,256]{2,1,0:T(8,128)S(1)} %get-tuple-element.61.refs_3_.own_t, ...), custom_call_target="tpu_custom_call" | custom-call | flops 805306368 | bytes 4849664 | tf_op jit(solution)/shard_map/pallas_call | solution.py:97
  71.6 3.8 %shard_map.80.refs_0_.grads = bf16[512,2048]{1,0:T(8,128)(2,1)} custom-call(bf16[64,2048]{1,0:T(8,128)(2,1)} %collective-permute-done.11.refs_0_, bf16[64,2048]{1,0:T(8,128)(2,1)} %collective-permute-done.12.refs_1_, bf16[64,2048]{1,0:T(8,128)(2,1)} %collective-permute-done.13.refs_2_, bf16[64,2048]{1,0:T(8,128)(2,1)} %collective-permute-done.14.refs_3_, ...), custom_call_target="tpu_custom_call" | custom-call | bytes 4194304 | tf_op jit(solution)/shard_map/pallas_call | solution.py:124
  84.5 3.6 %collective-permute-done.18.refs_4_.got_t = bf16[2,384,256]{2,1,0:T(8,128)(2,1)S(1)} collective-permute-done((bf16[2,384,256]{2,1,0:T(8,128)(2,1)}, bf16[2,384,256]{2,1,0:T(8,128)(2,1)S(1)}, u32[]{:S(2)}, u32[]{:S(2)}) %collective-permute-start.18) | collective-permute-done | bytes 393248 | tf_op jit(solution)/shard_map/ppermute | solution.py:245
  89.9 3.4 %shard_map.85 = (f32[2,384,256]{2,1,0:T(8,128)S(1)}, bf16[2,384,256]{2,1,0:T(8,128)(2,1)}) custom-call(bf16[512,2048]{1,0:T(8,128)(2,1)S(1)} %copy-done.8, bf16[2048,1792]{1,0:T(8,128)(2,1)} %refs_1_.32, bf16[2048,1792]{1,0:T(8,128)(2,1)} %refs_2_.19, f32[1,384,256]{2,1,0:T(8,128)S(1)} %get-tuple-element.65.refs_3_.own_g, bf16[2,384,256]{2,1,0:T(8,128)(2,1)S(1)} %copy-done.29), custom_call_target="tpu_custom_call" | custom-call | flops 805306368 | bytes 4849664 | tf_op jit(solution)/shard_map/pallas_call | solution.py:97
  95.6 4.1 %shard_map.95.flipped = bf16[2048,512]{1,0:T(8,128)(2,1)} custom-call(bf16[512,2048]{1,0:T(8,128)(2,1)} %shard_map.79.refs_0_.x_ref, f32[2,384,256]{2,1,0:T(8,128)} %copy-done.16), custom_call_target="tpu_custom_call" | custom-call | bytes 4194304 | tf_op jit(solution)/shard_map/pallas_call | solution.py:143
  104.4 2.7 %shard_map.87 = (f32[2,384,256]{2,1,0:T(8,128)S(1)}, bf16[2,384,256]{2,1,0:T(8,128)(2,1)S(1)}) custom-call(bf16[512,2048]{1,0:T(8,128)(2,1)S(1)} %copy-done.9, bf16[2048,1792]{1,0:T(8,128)(2,1)} %refs_1_.32, bf16[2048,1792]{1,0:T(8,128)(2,1)} %refs_2_.19, f32[1,384,256]{2,1,0:T(8,128)S(1)} %get-tuple-element.69.refs_3_.rest_0_.own_g, ...), custom_call_target="tpu_custom_call" | custom-call | flops 805306368 | bytes 4849664 | tf_op jit(solution)/shard_map/pallas_call | solution.py:97
  107.7 5.8 %shard_map.96 = (bf16[2048,1792]{1,0:T(8,128)(2,1)}, bf16[2048,1792]{1,0:T(8,128)(2,1)}, bf16[1792,2048]{1,0:T(8,128)(2,1)}) custom-call(f32[3,64,512]{2,1,0:T(8,128)S(1)} %copy-done.19, bf16[3,64,512]{2,1,0:T(8,128)(2,1)S(1)} %copy-done.21, f32[3,64,1792]{2,1,0:T(8,128)S(1)} %get-tuple-element.59.refs_3_.own_b, bf16[3,64,1792]{2,1,0:T(8,128)(2,1)S(1)} %copy-done.11, ...), custom_call_target="tpu_custom_call" | custom-call | flops 1610612736 | bytes 9699328 | tf_op jit(solution)/shard_map/pallas_call | solution.py:214
  117.0 2.7 %shard_map.89 = (f32[2,384,256]{2,1,0:T(8,128)S(1)}, bf16[2,384,256]{2,1,0:T(8,128)(2,1)S(1)}) custom-call(bf16[512,2048]{1,0:T(8,128)(2,1)S(1)} %copy-done.9, bf16[2048,1792]{1,0:T(8,128)(2,1)} %refs_1_.32, bf16[2048,1792]{1,0:T(8,128)(2,1)} %refs_2_.19, f32[1,384,256]{2,1,0:T(8,128)S(1)} %get-tuple-element.73.refs_3_.rest_3_.own_g, ...), custom_call_target="tpu_custom_call" | custom-call | flops 805306368 | bytes 4849664 | tf_op jit(solution)/shard_map/pallas_call | solution.py:97
  120.3 5.8 %shard_map.97 = (bf16[2048,1792]{1,0:T(8,128)(2,1)}, bf16[2048,1792]{1,0:T(8,128)(2,1)}, bf16[1792,2048]{1,0:T(8,128)(2,1)}) custom-call(f32[3,64,512]{2,1,0:T(8,128)S(1)} %copy-done.19, bf16[3,64,512]{2,1,0:T(8,128)(2,1)S(1)} %copy-done.21, ...), custom_call_target="tpu_custom_call", output_to_operand_aliasing={{0}: (10, {}), {1}: (11, {}), {2}: (12, {})} | custom-call | flops 1610612736 | bytes 9699328 | tf_op jit(solution)/shard_map/pallas_call | solution.py:214
  129.5 3.4 %shard_map.91 = (f32[2,384,256]{2,1,0:T(8,128)S(1)}, bf16[2,384,256]{2,1,0:T(8,128)(2,1)}) custom-call(bf16[512,2048]{1,0:T(8,128)(2,1)S(1)} %copy-done.9, bf16[2048,1792]{1,0:T(8,128)(2,1)} %refs_1_.32, bf16[2048,1792]{1,0:T(8,128)(2,1)} %refs_2_.19, f32[1,384,256]{2,1,0:T(8,128)S(1)} %get-tuple-element.77.refs_3_.rest_3_.own_g, ...), custom_call_target="tpu_custom_call" | custom-call | flops 805306368 | bytes 4849664 | tf_op jit(solution)/shard_map/pallas_call | solution.py:97
  133.5 5.9 %shard_map.98 = (bf16[2048,1792]{1,0:T(8,128)(2,1)}, bf16[2048,1792]{1,0:T(8,128)(2,1)}, bf16[1792,2048]{1,0:T(8,128)(2,1)}) custom-call(f32[3,64,1280]{2,1,0:T(8,128)S(1)} %copy-done.13, bf16[3,64,1280]{2,1,0:T(8,128)(2,1)S(1)} %copy-done.15, ...), custom_call_target="tpu_custom_call", output_to_operand_aliasing={{0}: (10, {}), {1}: (11, {}), {2}: (12, {})} | custom-call | flops 1610612736 | bytes 9699328 | tf_op jit(solution)/shard_map/pallas_call | solution.py:214
  146.0 5.8 %shard_map.99 = (bf16[2048,1792]{1,0:T(8,128)(2,1)}, bf16[2048,1792]{1,0:T(8,128)(2,1)}, bf16[1792,2048]{1,0:T(8,128)(2,1)}) custom-call(f32[3,64,1280]{2,1,0:T(8,128)S(1)} %copy-done.13, bf16[3,64,1280]{2,1,0:T(8,128)(2,1)S(1)} %copy-done.15, ...), custom_call_target="tpu_custom_call", output_to_operand_aliasing={{0}: (10, {}), {1}: (11, {}), {2}: (12, {})} | custom-call | flops 1610612736 | bytes 9699328 | tf_op jit(solution)/shard_map/pallas_call | solution.py:214
  155.1 5.6 %shard_map.100 = (bf16[2048,1792]{1,0:T(8,128)(2,1)}, bf16[2048,1792]{1,0:T(8,128)(2,1)}, bf16[1792,2048]{1,0:T(8,128)(2,1)}) custom-call(f32[3,64,1280]{2,1,0:T(8,128)S(1)} %copy-done.13, bf16[3,64,1280]{2,1,0:T(8,128)(2,1)S(1)} %copy-done.15, ...), custom_call_target="tpu_custom_call", output_to_operand_aliasing={{0}: (10, {}), {1}: (11, {}), {2}: (12, {})} | custom-call | flops 1610612736 | bytes 9699328 | tf_op jit(solution)/shard_map/pallas_call | solution.py:214
  160.7 5.6 %shard_map.101 = (bf16[2048,1792]{1,0:T(8,128)(2,1)}, bf16[2048,1792]{1,0:T(8,128)(2,1)}, bf16[1792,2048]{1,0:T(8,128)(2,1)}) custom-call(f32[3,64,1280]{2,1,0:T(8,128)S(1)} %copy-done.13, bf16[3,64,1280]{2,1,0:T(8,128)(2,1)S(1)} %copy-done.15, ...), custom_call_target="tpu_custom_call", output_to_operand_aliasing={{0}: (10, {}), {1}: (11, {}), {2}: (12, {})} | custom-call | flops 1610612736 | bytes 9699328 | tf_op jit(solution)/shard_map/pallas_call | solution.py:214
  166.4 5.6 %shard_map.102 = (bf16[2048,1792]{1,0:T(8,128)(2,1)}, bf16[2048,1792]{1,0:T(8,128)(2,1)}, bf16[1792,2048]{1,0:T(8,128)(2,1)}) custom-call(f32[3,64,1280]{2,1,0:T(8,128)S(1)} %copy-done.13, bf16[3,64,1280]{2,1,0:T(8,128)(2,1)S(1)} %copy-done.15, ...), custom_call_target="tpu_custom_call", output_to_operand_aliasing={{0}: (10, {}), {1}: (11, {}), {2}: (12, {})} | custom-call | flops 1610612736 | bytes 9699328 | tf_op jit(solution)/shard_map/pallas_call | solution.py:214
  (151 shorter events, 50.4 us)
Async XLA Ops:
  8.6 18.7 %collective-permute-start.2 = (bf16[64,2048]{1,0:T(8,128)(2,1)}, bf16[64,2048]{1,0:T(8,128)(2,1)S(1)}, u32[]{:S(2)}, u32[]{:S(2)}) collective-permute-start(bf16[64,2048]{1,0:T(8,128)(2,1)} %refs_6_.3), channel_id=1, source_target_pairs={{0,2},{2,0},{4,6},{6,4},{8,10},{10,8},{12,14},{14,12},{1,3},{3,1},... | collective-permute-start | bytes 786440 | tf_op jit(solution)/shard_map/ppermute | solution.py:248
  9.1 19.8 %collective-permute-start.7 = (bf16[64,2048]{1,0:T(8,128)(2,1)S(1)}, bf16[64,2048]{1,0:T(8,128)(2,1)S(1)}, u32[]{:S(2)}, u32[]{:S(2)}) collective-permute-start(bf16[64,2048]{1,0:T(8,128)(2,1)S(1)} %copy-done.27), channel_id=1, source_target_pairs={{0,12},{2,14},{4,0},{6,2},{8,4},{10,6},{12,8},{14,10},{1,13},{3,15... | collective-permute-start | bytes 786440 | tf_op jit(solution)/shard_map/ppermute | solution.py:252
  12.7 16.2 %collective-permute-start.5 = (bf16[64,2048]{1,0:T(8,128)(2,1)S(1)}, bf16[64,2048]{1,0:T(8,128)(2,1)S(1)}, u32[]{:S(2)}, u32[]{:S(2)}) collective-permute-start(bf16[64,2048]{1,0:T(8,128)(2,1)S(1)} %copy-done.27), channel_id=1, source_target_pairs={{0,4},{2,6},{4,8},{6,10},{8,12},{10,14},{12,0},{14,2},{1,5},{3,7},... | collective-permute-start | bytes 786440 | tf_op jit(solution)/shard_map/ppermute | solution.py:252
  13.5 27.3 %collective-permute-start.6 = (bf16[64,2048]{1,0:T(8,128)(2,1)S(1)}, bf16[64,2048]{1,0:T(8,128)(2,1)S(1)}, u32[]{:S(2)}, u32[]{:S(2)}) collective-permute-start(bf16[64,2048]{1,0:T(8,128)(2,1)S(1)} %copy-done.27), channel_id=1, source_target_pairs={{0,8},{2,10},{4,12},{6,14},{8,0},{10,2},{12,4},{14,6},{1,9},{3,11}... | collective-permute-start | bytes 786440 | tf_op jit(solution)/shard_map/ppermute | solution.py:252
  16.3 36.5 %collective-permute-start.11 = (bf16[64,2048]{1,0:T(8,128)(2,1)}, bf16[64,2048]{1,0:T(8,128)(2,1)}, u32[]{:S(2)}, u32[]{:S(2)}) collective-permute-start(bf16[64,2048]{1,0:T(8,128)(2,1)} %refs_6_.3), channel_id=1, source_target_pairs={{0,4},{2,6},{4,8},{6,10},{8,12},{10,14},{12,0},{14,2},{1,5},{3,7},... | collective-permute-start | bytes 786440 | tf_op jit(solution)/shard_map/ppermute | solution.py:252
  27.3 36.5 %collective-permute-start = (bf16[3,64,1280]{2,1,0:T(8,128)(2,1)}, bf16[3,64,1280]{2,1,0:T(8,128)(2,1)S(1)}, u32[]{:S(2)}, u32[]{:S(2)}) collective-permute-start(bf16[3,64,1280]{2,1,0:T(8,128)(2,1)} %get-tuple-element.57), channel_id=1, source_target_pairs={{0,1},{1,0},{2,3},{3,2},{4,5},{5,4},{6,7},{7,6},{8,9},{9,8},{10,11... | collective-permute-start | bytes 1474568 | tf_op jit(solution)/shard_map/ppermute | solution.py:245
  28.9 24.5 %collective-permute-start.10 = (bf16[64,2048]{1,0:T(8,128)(2,1)S(1)}, bf16[64,2048]{1,0:T(8,128)(2,1)S(1)}, u32[]{:S(2)}, u32[]{:S(2)}) collective-permute-start(bf16[64,2048]{1,0:T(8,128)(2,1)S(1)} %collective-permute-done.7.refs_2_), channel_id=1, source_target_pairs={{0,2},{2,0},{4,6},{6,4},{8,10},{10,8},{12,14},{14,12},{1,3},{3,1},... | collective-permute-start | bytes 786440 | tf_op jit(solution)/shard_map/ppermute | solution.py:248
  28.9 24.5 %collective-permute-start.8 = (bf16[64,2048]{1,0:T(8,128)(2,1)S(1)}, bf16[64,2048]{1,0:T(8,128)(2,1)S(1)}, u32[]{:S(2)}, u32[]{:S(2)}) collective-permute-start(bf16[64,2048]{1,0:T(8,128)(2,1)S(1)} %collective-permute-done.5.refs_0_), channel_id=1, source_target_pairs={{0,2},{2,0},{4,6},{6,4},{8,10},{10,8},{12,14},{14,12},{1,3},{3,1},... | collective-permute-start | bytes 786440 | tf_op jit(solution)/shard_map/ppermute | solution.py:248
  52.8 22.6 %collective-permute-start.4 = (bf16[3,64,1792]{2,1,0:T(8,128)(2,1)}, bf16[3,64,1792]{2,1,0:T(8,128)(2,1)S(1)}, u32[]{:S(2)}, u32[]{:S(2)}) collective-permute-start(bf16[3,64,1792]{2,1,0:T(8,128)(2,1)} %get-tuple-element.60), channel_id=1, source_target_pairs={{0,1},{1,0},{2,3},{3,2},{4,5},{5,4},{6,7},{7,6},{8,9},{9,8},{10,11... | collective-permute-start | bytes 2064392 | tf_op jit(solution)/shard_map/ppermute | solution.py:245
  53.4 15.3 %collective-permute-start.12 = (bf16[64,2048]{1,0:T(8,128)(2,1)}, bf16[64,2048]{1,0:T(8,128)(2,1)}, u32[]{:S(2)}, u32[]{:S(2)}) collective-permute-start(bf16[64,2048]{1,0:T(8,128)(2,1)} %refs_6_.3), channel_id=1, source_target_pairs={{0,8},{2,10},{4,12},{6,14},{8,0},{10,2},{12,4},{14,6},{1,9},{3,11}... | collective-permute-start | bytes 786440 | tf_op jit(solution)/shard_map/ppermute | solution.py:252
  53.4 15.9 %collective-permute-start.13 = (bf16[64,2048]{1,0:T(8,128)(2,1)}, bf16[64,2048]{1,0:T(8,128)(2,1)}, u32[]{:S(2)}, u32[]{:S(2)}) collective-permute-start(bf16[64,2048]{1,0:T(8,128)(2,1)} %refs_6_.3), channel_id=1, source_target_pairs={{0,12},{2,14},{4,0},{6,2},{8,4},{10,6},{12,8},{14,10},{1,13},{3,15... | collective-permute-start | bytes 786440 | tf_op jit(solution)/shard_map/ppermute | solution.py:252
  54.9 14.4 %collective-permute-start.14 = (bf16[64,2048]{1,0:T(8,128)(2,1)}, bf16[64,2048]{1,0:T(8,128)(2,1)}, u32[]{:S(2)}, u32[]{:S(2)}) collective-permute-start(bf16[64,2048]{1,0:T(8,128)(2,1)} %collective-permute-done.11.refs_0_), channel_id=1, source_target_pairs={{0,2},{2,0},{4,6},{6,4},{8,10},{10,8},{12,14},{14,12},{1,3},{3,1},... | collective-permute-start | bytes 786440 | tf_op jit(solution)/shard_map/ppermute | solution.py:248
  63.8 17.4 %collective-permute-start.17 = (bf16[2,384,256]{2,1,0:T(8,128)(2,1)}, bf16[2,384,256]{2,1,0:T(8,128)(2,1)}, u32[]{:S(2)}, u32[]{:S(2)}) collective-permute-start(bf16[2,384,256]{2,1,0:T(8,128)(2,1)} %get-tuple-element.64), channel_id=1, source_target_pairs={{0,1},{1,0},{2,3},{3,2},{4,5},{5,4},{6,7},{7,6},{8,9},{9,8},{10,11... | collective-permute-start | bytes 1179656 | tf_op jit(solution)/shard_map/ppermute | solution.py:245
  68.7 19.4 %collective-permute-start.18 = (bf16[2,384,256]{2,1,0:T(8,128)(2,1)}, bf16[2,384,256]{2,1,0:T(8,128)(2,1)S(1)}, u32[]{:S(2)}, u32[]{:S(2)}) collective-permute-start(bf16[2,384,256]{2,1,0:T(8,128)(2,1)} %get-tuple-element.66), channel_id=1, source_target_pairs={{0,1},{1,0},{2,3},{3,2},{4,5},{5,4},{6,7},{7,6},{8,9},{9,8},{10,11... | collective-permute-start | bytes 1179656 | tf_op jit(solution)/shard_map/ppermute | solution.py:245
  79.7 20.0 %collective-permute-start.19 = (bf16[1,384,256]{2,1,0:T(8,128)(2,1)}, bf16[1,384,256]{2,1,0:T(8,128)(2,1)}, u32[]{:S(2)}, u32[]{:S(2)}) collective-permute-start(bf16[1,384,256]{2,1,0:T(8,128)(2,1)} %get-tuple-element.68), channel_id=1, source_target_pairs={{0,1},{1,0},{2,3},{3,2},{4,5},{5,4},{6,7},{7,6},{8,9},{9,8},{10,11... | collective-permute-start | bytes 589832 | tf_op jit(solution)/shard_map/ppermute | solution.py:245
  83.8 20.6 %collective-permute-start.20 = (bf16[1,384,256]{2,1,0:T(8,128)(2,1)}, bf16[1,384,256]{2,1,0:T(8,128)(2,1)}, u32[]{:S(2)}, u32[]{:S(2)}) collective-permute-start(bf16[1,384,256]{2,1,0:T(8,128)(2,1)} %get-tuple-element.70), channel_id=1, source_target_pairs={{0,1},{1,0},{2,3},{3,2},{4,5},{5,4},{6,7},{7,6},{8,9},{9,8},{10,11... | collective-permute-start | bytes 589832 | tf_op jit(solution)/shard_map/ppermute | solution.py:245
  95.0 18.5 %collective-permute-start.21 = (bf16[2,384,256]{2,1,0:T(8,128)(2,1)}, bf16[2,384,256]{2,1,0:T(8,128)(2,1)}, u32[]{:S(2)}, u32[]{:S(2)}) collective-permute-start(bf16[2,384,256]{2,1,0:T(8,128)(2,1)} %get-tuple-element.72), channel_id=1, source_target_pairs={{0,1},{1,0},{2,3},{3,2},{4,5},{5,4},{6,7},{7,6},{8,9},{9,8},{10,11... | collective-permute-start | bytes 1179656 | tf_op jit(solution)/shard_map/ppermute | solution.py:245
  102.8 14.2 %collective-permute-start.22 = (bf16[1,384,256]{2,1,0:T(8,128)(2,1)S(1)}, bf16[1,384,256]{2,1,0:T(8,128)(2,1)S(1)}, u32[]{:S(2)}, u32[]{:S(2)}) collective-permute-start(bf16[1,384,256]{2,1,0:T(8,128)(2,1)S(1)} %get-tuple-element.74), channel_id=1, source_target_pairs={{0,1},{1,0},{2,3},{3,2},{4,5},{5,4},{6,7},{7,6},{8,9},{9,8},{10,11... | collective-permute-start | bytes 589832 | tf_op jit(solution)/shard_map/ppermute | solution.py:245
  107.1 19.0 %collective-permute-start.23 = (bf16[2,384,256]{2,1,0:T(8,128)(2,1)S(1)}, bf16[2,384,256]{2,1,0:T(8,128)(2,1)S(1)}, u32[]{:S(2)}, u32[]{:S(2)}) collective-permute-start(bf16[2,384,256]{2,1,0:T(8,128)(2,1)S(1)} %get-tuple-element.76), channel_id=1, source_target_pairs={{0,1},{1,0},{2,3},{3,2},{4,5},{5,4},{6,7},{7,6},{8,9},{9,8},{10,11... | collective-permute-start | bytes 1179656 | tf_op jit(solution)/shard_map/ppermute | solution.py:245
  119.7 19.8 %collective-permute-start.25 = (bf16[2,384,256]{2,1,0:T(8,128)(2,1)S(1)}, bf16[2,384,256]{2,1,0:T(8,128)(2,1)S(1)}, u32[]{:S(2)}, u32[]{:S(2)}) collective-permute-start(bf16[2,384,256]{2,1,0:T(8,128)(2,1)S(1)} %get-tuple-element.80), channel_id=1, source_target_pairs={{0,1},{1,0},{2,3},{3,2},{4,5},{5,4},{6,7},{7,6},{8,9},{9,8},{10,11... | collective-permute-start | bytes 1179656 | tf_op jit(solution)/shard_map/ppermute | solution.py:245
  127.9 14.9 %collective-permute-start.26 = (bf16[1,384,256]{2,1,0:T(8,128)(2,1)S(1)}, bf16[1,384,256]{2,1,0:T(8,128)(2,1)S(1)}, u32[]{:S(2)}, u32[]{:S(2)}) collective-permute-start(bf16[1,384,256]{2,1,0:T(8,128)(2,1)S(1)} %get-tuple-element.82), channel_id=1, source_target_pairs={{0,1},{1,0},{2,3},{3,2},{4,5},{5,4},{6,7},{7,6},{8,9},{9,8},{10,11... | collective-permute-start | bytes 589832 | tf_op jit(solution)/shard_map/ppermute | solution.py:245
  133.0 18.8 %collective-permute-start.28 = (bf16[2,384,256]{2,1,0:T(8,128)(2,1)}, bf16[2,384,256]{2,1,0:T(8,128)(2,1)S(1)}, u32[]{:S(2)}, u32[]{:S(2)}) collective-permute-start(bf16[2,384,256]{2,1,0:T(8,128)(2,1)} %get-tuple-element.85), channel_id=1, source_target_pairs={{0,1},{1,0},{2,3},{3,2},{4,5},{5,4},{6,7},{7,6},{8,9},{9,8},{10,11... | collective-permute-start | bytes 1179656 | tf_op jit(solution)/shard_map/ppermute | solution.py:245
  141.3 19.5 %collective-permute-start.30 = (bf16[1,384,256]{2,1,0:T(8,128)(2,1)S(1)}, bf16[1,384,256]{2,1,0:T(8,128)(2,1)S(1)}, u32[]{:S(2)}, u32[]{:S(2)}) collective-permute-start(bf16[1,384,256]{2,1,0:T(8,128)(2,1)S(1)} %get-tuple-element.88), channel_id=1, source_target_pairs={{0,1},{1,0},{2,3},{3,2},{4,5},{5,4},{6,7},{7,6},{8,9},{9,8},{10,11... | collective-permute-start | bytes 589832 | tf_op jit(solution)/shard_map/ppermute | solution.py:245
  145.4 21.0 %collective-permute-start.27 = (bf16[2,384,256]{2,1,0:T(8,128)(2,1)S(1)}, bf16[2,384,256]{2,1,0:T(8,128)(2,1)S(1)}, u32[]{:S(2)}, u32[]{:S(2)}) collective-permute-start(bf16[2,384,256]{2,1,0:T(8,128)(2,1)S(1)} %get-tuple-element.84), channel_id=1, source_target_pairs={{0,1},{1,0},{2,3},{3,2},{4,5},{5,4},{6,7},{7,6},{8,9},{9,8},{10,11... | collective-permute-start | bytes 1179656 | tf_op jit(solution)/shard_map/ppermute | solution.py:245
  (50 other events, 407.1 us)

commit v2 on v0

--- a/solution.py
+++ b/solution.py
@@ -1,7 +1,16 @@
+import functools
+
 import jax
 import jax.numpy as jnp
 from jax import lax
+from jax.experimental import pallas as pl
+from jax.experimental.pallas import tpu as pltpu
 from jax.sharding import PartitionSpec as P
+
+CHUNK = 256
+VMEM_LIMIT = 48 * 1024 * 1024
+F32, BF16 = jnp.float32, jnp.bfloat16
+SMALL_COST = pl.CostEstimate(flops=1024, bytes_accessed=1024, transcendentals=0)
 
 
 def contract_rows(left, right):
@@ -21,7 +30,7 @@
     return (hidden, gate_delta, up_delta)
 
 
-def shards(tokens, out_grad, gate_weight, up_weight, down_weight):
+def plain_shards(tokens, out_grad, gate_weight, up_weight, down_weight):
     token_rows, grad_rows = (
         lax.all_gather(tokens, "feat", axis=0, tiled=True),
         lax.all_gather(out_grad, "feat", axis=0, tiled=True),
@@ -31,16 +40,13 @@
     hidden_part = lax.dot_general(
         grad_rows, down_weight, (((1,), (1,)), ((), ())), preferred_element_type=jnp.float32
     )
-    gate, up = (
-        lax.psum_scatter(gate_part, "tok", scatter_dimension=0, tiled=True),
-        lax.psum_scatter(up_part, "tok", scatter_dimension=0, tiled=True),
-    )
-    grad_hidden = lax.psum_scatter(hidden_part, "tok", scatter_dimension=0, tiled=True)
-    hidden, gate_delta, up_delta = swiglu_parts(gate, up, grad_hidden)
+    gate, up, grad_hidden = (
+        lax.psum_scatter(part, "tok", scatter_dimension=0, tiled=True)
+        for part in (gate_part, up_part, hidden_part)
+    )
     hidden, gate_delta, up_delta = (
-        lax.all_gather(hidden, "tok", axis=0, tiled=True),
-        lax.all_gather(gate_delta, "tok", axis=0, tiled=True),
-        lax.all_gather(up_delta, "tok", axis=0, tiled=True),
+        lax.all_gather(part, "tok", axis=0, tiled=True)
+        for part in swiglu_parts(gate, up, grad_hidden)
     )
     grad_gate = contract_rows(token_rows, gate_delta).astype(jnp.bfloat16)
     grad_up = contract_rows(token_rows, up_delta).astype(jnp.bfloat16)
@@ -48,9 +54,280 @@
     return (grad_gate, grad_up, grad_down)
 
 
+def rows_of(refs):
+    parts = [ref[...] for ref in refs]
+    return parts[0] if len(parts) == 1 else jnp.concatenate(parts, axis=0)
+
+
+def partial_kernel(n_pieces, n_token, n_grad, *refs):
+    refs = list(refs)
+    own_ref, send_ref = refs[-2:]
+    if n_token:
+        rows = rows_of([refs.pop(0) for _ in range(n_pieces)])
+        for i in range(n_token):
+            part = jnp.dot(rows, refs.pop(0)[...], preferred_element_type=F32)
+            own_ref[i] = part
+            send_ref[i] = part.astype(BF16)
+    if n_grad:
+        rows = rows_of([refs.pop(0) for _ in range(n_pieces)])
+        part = lax.dot_general(
+            rows, refs.pop(0)[...], (((1,), (1,)), ((), ())), preferred_element_type=F32
+        )
+        own_ref[n_token] = part
+        send_ref[n_token] = part.astype(BF16)
+
+
+def partial_products(rows, grad_rows, heights, weights, down, first, width, after):
+    n_token, n_grad = len(weights), 0 if down is None else 1
+    n_rows = sum(heights)
+    depth = (rows or grad_rows)[0].shape[1]
+    start, count = first // CHUNK, width // CHUNK
+    piece_specs = [pl.BlockSpec((h, depth), lambda i: (0, 0)) for h in heights]
+    args, specs = [], []
+    if n_token:
+        args += rows
+        specs += piece_specs
+        for w in weights:
+            args.append(w)
+            specs.append(pl.BlockSpec((depth, CHUNK), lambda i: (0, start + i)))
+    if n_grad:
+        args += grad_rows
+        specs += piece_specs
+        args.append(down)
+        specs.append(pl.BlockSpec((CHUNK, depth), lambda i: (start + i, 0)))
+    for a in after:
+        args.append(a)
+        specs.append(pl.BlockSpec(memory_space=pl.ANY))
+    n = n_token + n_grad
+    block = pl.BlockSpec((n, n_rows, CHUNK), lambda i: (0, 0, i))
+    shape = (n, n_rows, width)
+    return pl.pallas_call(
+        functools.partial(partial_kernel, len(heights), n_token, n_grad),
+        grid=(count,),
+        in_specs=specs,
+        out_specs=[block, block],
+        out_shape=[jax.ShapeDtypeStruct(shape, F32), jax.ShapeDtypeStruct(shape, BF16)],
+        compiler_params=pltpu.CompilerParams(vmem_limit_bytes=VMEM_LIMIT),
+        cost_estimate=SMALL_COST,
+    )(*args)
+
+
+def join_kernel(n_pieces, n_after, *refs):
+    refs = refs[:n_pieces] + refs[n_pieces + n_after :]
+    out_ref, base = refs[n_pieces], 0
+    for ref in refs[:n_pieces]:
+        n = ref.shape[0]
+        out_ref[base : base + n, :] = ref[...]
+        base += n
+    if len(refs) > n_pieces + 1:
+        refs[-1][...] = out_ref[...].T
+
+
+def join(pieces, flip, after):
+    n_rows = sum(p.shape[0] for p in pieces)
+    depth = pieces[0].shape[1]
+    tile = depth // 2
+    out_specs = [pl.BlockSpec((n_rows, tile), lambda i: (0, i))]
+    out_shape = [jax.ShapeDtypeStruct((n_rows, depth), BF16)]
+    if flip:
+        out_specs.append(pl.BlockSpec((tile, n_rows), lambda i: (i, 0)))
+        out_shape.append(jax.ShapeDtypeStruct((depth, n_rows), BF16))
+    return pl.pallas_call(
+        functools.partial(join_kernel, len(pieces), len(after)),
+        grid=(2,),
+        in_specs=[pl.BlockSpec((p.shape[0], tile), lambda i: (0, i)) for p in pieces]
+        + [pl.BlockSpec(memory_space=pl.ANY)] * len(after),
+        out_specs=out_specs,
+        out_shape=out_shape,
+        compiler_params=pltpu.CompilerParams(vmem_limit_bytes=VMEM_LIMIT),
+        cost_estimate=SMALL_COST,
+    )(*pieces, *after)
+
+
+def others_kernel(n_own, blocks_ref, *refs):
+    n_chips = blocks_ref.shape[0] // n_own
+    chip = lax.axis_index("feat") // 2
+    for k in range(1, n_chips):
+        row = pl.multiple_of(lax.rem(chip + k, n_chips) * n_own, n_own)
+        refs[-1][(k - 1) * n_own : k * n_own, :] = blocks_ref[pl.ds(row, n_own), :]
+
+
+def others(blocks, n_own, after):
+    n_rows, depth = blocks.shape
+    tile = depth // 2
+    return pl.pallas_call(
+        functools.partial(others_kernel, n_own),
+        grid=(2,),
+        in_specs=[pl.BlockSpec((n_rows, tile), lambda i: (0, i))]
+        + [pl.BlockSpec(memory_space=pl.ANY)] * len(after),
+        out_specs=pl.BlockSpec((n_rows - n_own, tile), lambda i: (0, i)),
+        out_shape=jax.ShapeDtypeStruct((n_rows - n_own, depth), BF16),
+        compiler_params=pltpu.CompilerParams(vmem_limit_bytes=VMEM_LIMIT),
+        cost_estimate=SMALL_COST,
+    )(blocks, *after)
+
+
+def grads_kernel(own_a, got_a, own_t, got_t, own_g, got_g, flipped, grads, *rest):
+    gg_ref, gu_ref, gd_ref, hidden_t, gate_delta, up_delta = rest[-6:]
+
+    @pl.when(pl.program_id(0) == 0)
+    def _():
+        def total(own, got, i):
+            return own[i] + got[i].astype(F32)
+
+        base = 0
+        for gate, up, grad_hidden in (
+            (
+                total(own_t, got_t, 0),
+                total(own_t, got_t, 1),
+                total(own_g, got_g, own_g.shape[0] - 1),
+            ),
+            tuple(total(own_a, got_a, i) for i in range(3)),
+        ):
+            sigmoid_gate = jax.nn.sigmoid(gate)
+            activated = gate * sigmoid_gate
+            n = gate.shape[0]
+            hidden_t[:, base : base + n] = (activated * up).astype(BF16).T
+            gate_delta[base : base + n, :] = (
+                grad_hidden * up * sigmoid_gate * (1.0 + gate * (1.0 - sigmoid_gate))
+            ).astype(BF16)
+            up_delta[base : base + n, :] = (grad_hidden * activated).astype(BF16)
+            base += n
+
+    gg_ref[...] = jnp.dot(flipped[...], gate_delta[...], preferred_element_type=F32).astype(BF16)
+    gu_ref[...] = jnp.dot(flipped[...], up_delta[...], preferred_element_type=F32).astype(BF16)
+    gd_ref[...] = jnp.dot(hidden_t[...], grads[...], preferred_element_type=F32).astype(BF16)
+
+
+def group_grads(
+    first, width, a, a_first, t, g, far_first, flipped, grads, hidden_units, so_far, after
+):
+    depth, n_tokens = flipped.shape
+    steps = 4
+    tile = depth // steps
+    j, far = first // width, far_first // width
+
+    def part(arr, offset):
+        return pl.BlockSpec(
+            (arr.shape[0], arr.shape[1], width), lambda i: (0, 0, offset // width)
+        )
+
+    g_block = pl.BlockSpec((1, g[0].shape[1], width), lambda i: (g[0].shape[0] - 1, 0, far))
+    t_block = pl.BlockSpec((2, t[0].shape[1], width), lambda i: (0, 0, far))
+    args = [a[0], a[1], t[0], t[1], g[0], g[1], flipped, grads]
+    specs = [part(a[0], a_first), part(a[1], a_first), t_block, t_block, g_block, g_block]
+    specs += [
+        pl.BlockSpec((tile, n_tokens), lambda i: (i, 0)),
+        pl.BlockSpec((n_tokens, tile), lambda i: (0, i)),
+    ]
+    aliases = {}
+    if so_far is not None:
+        for k, arr in enumerate(so_far):
+            aliases[len(args)] = k
+            args.append(arr)
+            specs.append(pl.BlockSpec(memory_space=pl.ANY))
+    for arr in after:
+        args.append(arr)
+        specs.append(pl.BlockSpec(memory_space=pl.ANY))
+    up_shape = jax.ShapeDtypeStruct((depth, hidden_units), BF16)
+    down_shape = jax.ShapeDtypeStruct((hidden_units, depth), BF16)
+    return pl.pallas_call(
+        grads_kernel,
+        grid=(steps,),
+        in_specs=specs,
+        out_specs=[
+            pl.BlockSpec((tile, width), lambda i: (i, j)),
+            pl.BlockSpec((tile, width), lambda i: (i, j)),
+            pl.BlockSpec((width, tile), lambda i: (j, i)),
+        ],
+        out_shape=[up_shape, up_shape, down_shape],
+        scratch_shapes=[
+            pltpu.VMEM((width, n_tokens), BF16),
+            pltpu.VMEM((n_tokens, width), BF16),
+            pltpu.VMEM((n_tokens, width), BF16),
+        ],
+        input_output_aliases=aliases,
+        compiler_params=pltpu.CompilerParams(vmem_limit_bytes=VMEM_LIMIT),
+        cost_estimate=SMALL_COST,
+    )(*args)
+
+
+def pair_shards(n_feat, tokens, out_grad, gate_weight, up_weight, down_weight):
+    hidden_units = gate_weight.shape[1]
+    weights = (gate_weight, up_weight)
+    wide = 2 * CHUNK
+    n_own = tokens.shape[0]
+    partial = partial_products
+
+    def swap(x):
+        return lax.ppermute(x, "tok", [(0, 1), (1, 0)])
+
+    def sibling(x):
+        return lax.ppermute(x, "feat", [(i, i ^ 1) for i in range(n_feat)])
+
+    def gather(x):
+        return lax.all_gather(
+            x, "feat", axis=0, tiled=True,
+            axis_index_groups=[list(range(c, n_feat, 2)) for c in range(2)],
+        )
+
+    near_tokens = [tokens, sibling(tokens)]
+    near_grad = [out_grad, sibling(out_grad)]
+    token_blocks, grad_blocks = gather(tokens), gather(out_grad)
+    near = (n_own, n_own)
+    far = ((n_feat - 2) * n_own,)
+
+    def near_part(first, width, after):
+        own, send = partial(
+            near_tokens, near_grad, near, weights, down_weight, first, width, after
+        )
+        return own, swap(send)
+
+    def far_part(first, width, kinds, after):
+        own, send = partial(
+            [all_tokens] if "t" in kinds else None,
+            [all_grad] if "g" in kinds else None,
+            far,
+            weights if "t" in kinds else (),
+            down_weight if "g" in kinds else None,
+            first, width, after,
+        )
+        return own, swap(send)
+
+    def joined(blocks, near_pieces, flip, after):
+        mine = others(blocks, n_own, after)
+        return join([mine, sibling(mine)] + near_pieces, flip, ())
+
+    a0 = near_part(0, wide, ())
+    a1 = near_part(wide, hidden_units - wide, (a0[0],))
+    all_tokens, flipped = joined(token_blocks, near_tokens, True, (a1[0], a0[1]))
+    t0 = far_part(0, wide, "t", (a1[1],))
+    t1 = far_part(wide, wide, "t", (t0[0],))
+    all_grad = joined(grad_blocks, near_grad, False, (t1[0], t0[1]))[0]
+    g0 = far_part(0, wide, "g", (t1[0],))
+    g1 = far_part(wide, wide, "g", (g0[0], t1[1]))
+    f2 = far_part(2 * wide, wide, "tg", (g1[0], g0[1]))
+    f3 = far_part(3 * wide, hidden_units - 3 * wide, "tg", (f2[0], g1[1]))
+
+    outs = None
+    for first, width, a, a_first, t, g, far_first, after in (
+        (0, wide, a0, 0, t0, g0, 0, (f2[0],)),
+        (wide, wide, a1, 0, t1, g1, 0, (f3[0],)),
+        (2 * wide, wide, a1, wide, f2, f2, 0, ()),
+        (3 * wide, hidden_units - 3 * wide, a1, 2 * wide, f3, f3, 0, ()),
+    ):
+        outs = group_grads(
+            first, width, a, a_first, t, g, far_first, flipped, all_grad, hidden_units,
+            outs, after,
+        )
+    return tuple(outs)
+
+
 def solution(mesh):
+    n_feat, n_tok = mesh.shape["feat"], mesh.shape["tok"]
+    pair = n_tok == 2 and n_feat % 2 == 0 and 2 < n_feat <= 8
     return jax.shard_map(
-        shards,
+        functools.partial(pair_shards, n_feat) if pair else plain_shards,
         mesh=mesh,
         in_specs=(
             P(("groups", "feat"), "tok"),

time: 342 us -> 191 us (0.56)
  waiting for transfers between devices: 248 us -> 82.5 us
  Pallas kernels: 0 us -> 71.4 us
  matrix products: 50.9 us -> 0 us
  local copies, waits for them, and re-layouts: 21.7 us -> 12.8 us
  starting transfers between devices: 0.5 us -> 9.09 us
  other arithmetic: 5.03 us -> 0 us
    reduce_scatter x3 -> x0, waiting for transfers between devices: 145 us -> none  [the longest x1 51.9 us: shards(): lax.psum_scatter(gate_part, 'tok', scatter_dimension=0, tiled=True)]
    all_gather x5 -> x2, waiting for transfers between devices: 101 us -> 18.5 us  [gather(): lax.all_gather(x, 'feat', axis=0, tiled=True, axis_index_groups=[list(ran...]
    pallas_call x0 -> x16, Pallas kernels: none -> 71.4 us  [the longest x8 38.1 us: partial_products(): pl.pallas_call(functools.partial(partial_kernel, len(heights), n_token, n...]
    ppermute x0 -> x12, waiting for transfers between devices: none -> 63.3 us  [the longest x8 57.7 us: swap(): return lax.ppermute(x, 'tok', [(0, 1), (1, 0)])]
    dot_general x6 -> x0, matrix products: 50.9 us -> none  [the longest x3 22.7 us: contract_rows(): lax.dot_general(left, right, (((0,), (0,)), ((), ())), preferred_element_...]
    ppermute x0 -> x12, starting transfers between devices: none -> 9.01 us  [the longest x8 8.34 us: swap(): return lax.ppermute(x, 'tok', [(0, 1), (1, 0)])]
    unnamed x6 -> x58, local copies, waits for them, and re-layouts: 21.7 us -> 12.8 us
    convert_element_type x1 -> x0, other arithmetic: 5.03 us -> none  [swiglu_parts(): hidden = (activated * up).astype(jnp.bfloat16)]
  transfers between devices with their start and end apart: 8 -> 14, of which waited for: 8 -> 11; matrix products, arithmetic and copies ran while one was open for 19% -> 0% of each run, Pallas kernels for 0% -> 31%
where the time goes in v2:
time: 191 us; the launch traced here: 190 us
  waiting for transfers between devices  82.5 us (43%)
  Pallas kernels  71.4 us (37%)
  between operations  14.2 us (7%)
  local copies, waits for them, and re-layouts  12.8 us (7%)
  starting transfers between devices  9.09 us (5%)
    ppermute x8, waiting for transfers between devices, swap(): return lax.ppermute(x, 'tok', [(0, 1), (1, 0)])  57.7 us
    pallas_call x8, Pallas kernels, partial_products(): pl.pallas_call(functools.partial(partial_kernel, len(heights), n_token, n...  38.1 us
    pallas_call x4, Pallas kernels, group_grads(): pl.pallas_call(grads_kernel, grid=(steps,), in_specs=specs, out_specs=[pl...  28.7 us
    all_gather x2, waiting for transfers between devices, gather(): lax.all_gather(x, 'feat', axis=0, tiled=True, axis_index_groups=[list(ran...  18.5 us
    unnamed x58, local copies, waits for them, and re-layouts  12.8 us
    ppermute x8, starting transfers between devices, swap(): return lax.ppermute(x, 'tok', [(0, 1), (1, 0)])  8.34 us
    ppermute x4, waiting for transfers between devices, sibling(): return lax.ppermute(x, 'feat', [(i, i ^ 1) for i in range(n_feat)])  5.64 us
  transfers between devices with their start and end apart: 14, of which 11 were waited for; matrix products, arithmetic and copies ran while one was open for 0% of the time, Pallas kernels for 31%

profile of v2, /device:TPU:0, one launch (start us, length us, event | category | flops | bytes accessed | tf_op | source)
XLA Modules:
  0.0 190.0 jit_solution(17693362708507235267)
XLA Ops:
  12.1 3.8 %shard_map.76 = (f32[3,128,512]{2,1,0:T(8,128)S(1)}, bf16[3,128,512]{2,1,0:T(8,128)(2,1)S(1)}) custom-call(bf16[64,2048]{1,0:T(8,128)(2,1)S(1)} %copy-done.11, bf16[64,2048]{1,0:T(8,128)(2,1)S(1)} %collective-permute-done.refs_1_.refs_3_, bf16[2048,1792]{1,0:T(8,128)(2,1)} %refs_1_.11, bf16[2048,1792]{1,0:T(8,128)(2,1)} %refs_2_.15, ...), custom_call_target="tpu_custom_call" | custom-call | flops 1024 | bytes 1024 | tf_op jit(solution)/shard_map/pallas_call | solution.py:104
  15.9 2.9 %collective-permute-start.3 = (bf16[3,128,512]{2,1,0:T(8,128)(2,1)S(1)}, bf16[3,128,512]{2,1,0:T(8,128)(2,1)S(1)}, u32[]{:S(2)}, u32[]{:S(2)}) collective-permute-start(bf16[3,128,512]{2,1,0:T(8,128)(2,1)S(1)} %get-tuple-element.33), channel_id=1, source_target_pairs={{0,1},{1,0},{2,3},{3,2},{4,5},{5,4},{6,7},{7,6},{8,9},{9,8},{10,11... | collective-permute-start | bytes 1179656 | tf_op jit(solution)/shard_map/ppermute | solution.py:263
  18.9 9.3 %shard_map.77 = (f32[3,128,1280]{2,1,0:T(8,128)S(1)}, bf16[3,128,1280]{2,1,0:T(8,128)(2,1)}) custom-call(bf16[64,2048]{1,0:T(8,128)(2,1)S(1)} %copy-done.11, bf16[64,2048]{1,0:T(8,128)(2,1)S(1)} %collective-permute-done.refs_1_.refs_3_, bf16[2048,1792]{1,0:T(8,128)(2,1)} %refs_1_.11, bf16[2048,1792]{1,0:T(8,128)(2,1)} %refs_2_.15, ...), custom_call_target="tpu_custom_call" | custom-call | flops 1024 | bytes 1024 | tf_op jit(solution)/shard_map/pallas_call | solution.py:104
  29.2 11.1 %all-gather.3.cloned.1.call-done.blocks_ref = bf16[256,2048]{1,0:T(8,128)(2,1)} async-done(((bf16[64,2048]{1,0:T(8,128)(2,1)}), bf16[256,2048]{1,0:T(8,128)(2,1)}) %all-gather.3.cloned.1.call-update) | async-done | bytes 1048592 | tf_op jit(solution)/shard_map/all_gather | solution.py:269
  43.5 2.6 %collective-permute-done.4.refs_1_ = bf16[192,2048]{1,0:T(8,128)(2,1)} collective-permute-done((bf16[192,2048]{1,0:T(8,128)(2,1)}, bf16[192,2048]{1,0:T(8,128)(2,1)}, u32[]{:S(2)}, u32[]{:S(2)}) %collective-permute-start.4) | collective-permute-done | bytes 786464 | tf_op jit(solution)/shard_map/ppermute | solution.py:266
  47.0 2.9 %shard_map.79 = (bf16[512,2048]{1,0:T(8,128)(2,1)S(1)}, bf16[2048,512]{1,0:T(8,128)(2,1)}) custom-call(bf16[192,2048]{1,0:T(8,128)(2,1)} %shard_map.78.refs_0_, bf16[192,2048]{1,0:T(8,128)(2,1)} %collective-permute-done.4.refs_1_, bf16[64,2048]{1,0:T(8,128)(2,1)S(1)} %copy-done.12, bf16[64,2048]{1,0:T(8,128)(2,1)S(1)} %copy-done.22), custom_call_target="tpu_custom_call" | custom-call | flops 1024 | bytes 1024 | tf_op jit(solution)/shard_map/pallas_call | solution.py:135
  49.9 1.9 %collective-permute-done.2.refs_3_.got_a = bf16[3,128,1280]{2,1,0:T(8,128)(2,1)S(1)} collective-permute-done((bf16[3,128,1280]{2,1,0:T(8,128)(2,1)}, bf16[3,128,1280]{2,1,0:T(8,128)(2,1)S(1)}, u32[]{:S(2)}, u32[]{:S(2)}) %collective-permute-start.2) | collective-permute-done | bytes 983072 | tf_op jit(solution)/shard_map/ppermute | solution.py:263
  51.8 4.4 %shard_map.80 = (f32[2,384,512]{2,1,0:T(8,128)S(1)}, bf16[2,384,512]{2,1,0:T(8,128)(2,1)}) custom-call(bf16[512,2048]{1,0:T(8,128)(2,1)S(1)} %get-tuple-element.34.refs_0_, bf16[2048,1792]{1,0:T(8,128)(2,1)} %refs_1_.11, bf16[2048,1792]{1,0:T(8,128)(2,1)} %refs_2_.15, bf16[3,128,1280]{2,1,0:T(8,128)(2,1)S(1)} %collective-permute-done.2.refs_3_.got_a), custom_call_target="tpu_custom_call" | custom-call | flops 1024 | bytes 1024 | tf_op jit(solution)/shard_map/pallas_call | solution.py:104
  56.8 3.8 %shard_map.81 = (f32[2,384,512]{2,1,0:T(8,128)S(1)}, bf16[2,384,512]{2,1,0:T(8,128)(2,1)S(1)}) custom-call(bf16[512,2048]{1,0:T(8,128)(2,1)S(1)} %get-tuple-element.34.refs_0_, bf16[2048,1792]{1,0:T(8,128)(2,1)} %refs_1_.11, bf16[2048,1792]{1,0:T(8,128)(2,1)} %refs_2_.15, f32[2,384,512]{2,1,0:T(8,128)S(1)} %get-tuple-element.35.refs_3_.own_t), custom_call_target="tpu_custom_call" | custom-call | flops 1024 | bytes 1024 | tf_op jit(solution)/shard_map/pallas_call | solution.py:104
  63.8 7.5 %all-gather.5.cloned.1.call-done.blocks_ref = bf16[256,2048]{1,0:T(8,128)(2,1)} async-done(((bf16[64,2048]{1,0:T(8,128)(2,1)}), bf16[256,2048]{1,0:T(8,128)(2,1)}) %all-gather.5.cloned.1.call-update) | async-done | bytes 1048592 | tf_op jit(solution)/shard_map/all_gather | solution.py:269
  71.2 3.8 %collective-permute-done.5.refs_1_.got_t = bf16[2,384,512]{2,1,0:T(8,128)(2,1)} collective-permute-done((bf16[2,384,512]{2,1,0:T(8,128)(2,1)}, bf16[2,384,512]{2,1,0:T(8,128)(2,1)}, u32[]{:S(2)}, u32[]{:S(2)}) %collective-permute-start.5) | collective-permute-done | bytes 786464 | tf_op jit(solution)/shard_map/ppermute | solution.py:263
  75.0 1.4 copy-done.5
  78.9 1.4 collective-permute-done.6.refs_1_
  81.7 3.3 %shard_map.84 = (f32[1,384,512]{2,1,0:T(8,128)S(1)}, bf16[1,384,512]{2,1,0:T(8,128)(2,1)S(1)}) custom-call(bf16[512,2048]{1,0:T(8,128)(2,1)S(1)} %shard_map.83.refs_0_.refs_3_.grads, bf16[1792,2048]{1,0:T(8,128)(2,1)} %refs_4_.7, f32[2,384,512]{2,1,0:T(8,128)S(1)} %copy-done.6), custom_call_target="tpu_custom_call" | custom-call | flops 1024 | bytes 1024 | tf_op jit(solution)/shard_map/pallas_call | solution.py:104
  85.9 12.7 %collective-permute-done.7.refs_3_.got_t = bf16[2,384,512]{2,1,0:T(8,128)(2,1)S(1)} collective-permute-done((bf16[2,384,512]{2,1,0:T(8,128)(2,1)}, bf16[2,384,512]{2,1,0:T(8,128)(2,1)S(1)}, u32[]{:S(2)}, u32[]{:S(2)}) %collective-permute-start.7) | collective-permute-done | bytes 786464 | tf_op jit(solution)/shard_map/ppermute | solution.py:263
  98.6 2.8 %shard_map.85 = (f32[1,384,512]{2,1,0:T(8,128)S(1)}, bf16[1,384,512]{2,1,0:T(8,128)(2,1)S(1)}) custom-call(bf16[512,2048]{1,0:T(8,128)(2,1)S(1)} %shard_map.83.refs_0_.refs_3_.grads, bf16[1792,2048]{1,0:T(8,128)(2,1)} %refs_4_.7, f32[1,384,512]{2,1,0:T(8,128)S(1)} %get-tuple-element.38.refs_2_.own_g, ...), custom_call_target="tpu_custom_call" | custom-call | flops 1024 | bytes 1024 | tf_op jit(solution)/shard_map/pallas_call | solution.py:104
  101.5 5.1 %collective-permute-done.8.refs_6_.got_g = bf16[1,384,512]{2,1,0:T(8,128)(2,1)S(1)} collective-permute-done((bf16[1,384,512]{2,1,0:T(8,128)(2,1)S(1)}, bf16[1,384,512]{2,1,0:T(8,128)(2,1)S(1)}, u32[]{:S(2)}, u32[]{:S(2)}) %collective-permute-start.8) | collective-permute-done | bytes 393248 | tf_op jit(solution)/shard_map/ppermute | solution.py:263
  106.6 6.8 %shard_map.86 = (f32[3,384,512]{2,1,0:T(8,128)}, bf16[3,384,512]{2,1,0:T(8,128)(2,1)}) custom-call(bf16[512,2048]{1,0:T(8,128)(2,1)S(1)} %get-tuple-element.34.refs_0_, bf16[2048,1792]{1,0:T(8,128)(2,1)} %refs_1_.11, bf16[2048,1792]{1,0:T(8,128)(2,1)} %refs_2_.15, bf16[512,2048]{1,0:T(8,128)(2,1)} %copy-done, bf16[1792,2048]{1,0:T(8,128)(2,1)} %refs_4_.7, ...), custom_call_target="tpu_custom_call" | custom-call | flops 1024 | bytes 1024 | tf_op jit(solution)/shard_map/pallas_call | solution.py:104
  115.5 34.1 %collective-permute-done.9.refs_6_.got_g = bf16[1,384,512]{2,1,0:T(8,128)(2,1)S(1)} collective-permute-done((bf16[1,384,512]{2,1,0:T(8,128)(2,1)S(1)}, bf16[1,384,512]{2,1,0:T(8,128)(2,1)S(1)}, u32[]{:S(2)}, u32[]{:S(2)}) %collective-permute-start.9) | collective-permute-done | bytes 393248 | tf_op jit(solution)/shard_map/ppermute | solution.py:263
  149.7 3.9 %shard_map.87 = (f32[3,384,256]{2,1,0:T(8,128)S(1)}, bf16[3,384,256]{2,1,0:T(8,128)(2,1)S(1)}) custom-call(bf16[512,2048]{1,0:T(8,128)(2,1)S(1)} %get-tuple-element.34.refs_0_, bf16[2048,1792]{1,0:T(8,128)(2,1)} %refs_1_.11, bf16[2048,1792]{1,0:T(8,128)(2,1)} %refs_2_.15, bf16[512,2048]{1,0:T(8,128)(2,1)} %copy-done, bf16[1792,2048]{1,0:T(8,128)(2,1)} %refs_4_.7, ...), custom_call_target="tpu_custom_call" | custom-call | flops 1024 | bytes 1024 | tf_op jit(solution)/shard_map/pallas_call | solution.py:104
  154.5 7.4 %shard_map.88 = (bf16[2048,1792]{1,0:T(8,128)(2,1)}, bf16[2048,1792]{1,0:T(8,128)(2,1)}, bf16[1792,2048]{1,0:T(8,128)(2,1)}) custom-call(f32[3,128,512]{2,1,0:T(8,128)S(1)} %copy-done.14, bf16[3,128,512]{2,1,0:T(8,128)(2,1)S(1)} %copy-done.25, f32[2,384,512]{2,1,0:T(8,128)S(1)} %copy-done.8, bf16[2,384,512]{2,1,0:T(8,128)(2,1)} %collective-permute-done.5.refs_1_.got_t, ...), custom_call_target="tpu_custom_call" | custom-call | flops 1024 | bytes 1024 | tf_op jit(solution)/shard_map/pallas_call | solution.py:234
  162.0 7.6 %shard_map.89 = (bf16[2048,1792]{1,0:T(8,128)(2,1)}, bf16[2048,1792]{1,0:T(8,128)(2,1)}, bf16[1792,2048]{1,0:T(8,128)(2,1)}) custom-call(f32[3,128,1280]{2,1,0:T(8,128)} %copy-done.2, bf16[3,128,1280]{2,1,0:T(8,128)(2,1)S(1)} %collective-permute-done.2.refs_3_.got_a, ...), custom_call_target="tpu_custom_call", output_to_operand_aliasing={{0}: (8, {}), {1}: (9, {}), {2}: (10, {})} | custom-call | flops 1024 | bytes 1024 | tf_op jit(solution)/shard_map/pallas_call | solution.py:234
  169.6 8.1 %shard_map.90 = (bf16[2048,1792]{1,0:T(8,128)(2,1)}, bf16[2048,1792]{1,0:T(8,128)(2,1)}, bf16[1792,2048]{1,0:T(8,128)(2,1)}) custom-call(f32[3,128,1280]{2,1,0:T(8,128)S(1)} %copy-done.3, bf16[3,128,1280]{2,1,0:T(8,128)(2,1)S(1)} %collective-permute-done.2.refs_3_.got_a, ...), custom_call_target="tpu_custom_call", output_to_operand_aliasing={{0}: (8, {}), {1}: (9, {}), {2}: (10, {})} | custom-call | flops 1024 | bytes 1024 | tf_op jit(solution)/shard_map/pallas_call | solution.py:234
  177.7 5.5 %shard_map.91 = (bf16[2048,1792]{1,0:T(8,128)(2,1)}, bf16[2048,1792]{1,0:T(8,128)(2,1)}, bf16[1792,2048]{1,0:T(8,128)(2,1)}) custom-call(f32[3,128,1280]{2,1,0:T(8,128)S(1)} %copy-done.3, bf16[3,128,1280]{2,1,0:T(8,128)(2,1)S(1)} %collective-permute-done.2.refs_3_.got_a, ...), custom_call_target="tpu_custom_call", output_to_operand_aliasing={{0}: (8, {}), {1}: (9, {}), {2}: (10, {})} | custom-call | flops 1024 | bytes 1024 | tf_op jit(solution)/shard_map/pallas_call | solution.py:234
  (80 shorter events, 21.7 us)
Async XLA Ops:
  7.2 33.1 %all-gather.3.cloned.1.call-start = ((), (), s32[]{:S(2)}) async-start(), calls=%async_computation | async-start | bytes 1310720 | tf_op jit(solution)/shard_map/all_gather | solution.py:269
  7.9 63.3 %all-gather.5.cloned.1.call-start = ((), (), s32[]{:S(2)}) async-start(), calls=%async_computation.1 | async-start | bytes 1310720 | tf_op jit(solution)/shard_map/all_gather | solution.py:269
  7.9 1.9 collective-permute-start
  8.5 1.7 collective-permute-start.1
  9.8 9.0 %copy-start.21 = (bf16[64,2048]{1,0:T(8,128)(2,1)}, bf16[64,2048]{1,0:T(8,128)(2,1)S(1)}, u32[]{:S(2)}) copy-start(bf16[64,2048]{1,0:T(8,128)(2,1)S(1)} %collective-permute-done.refs_1_.refs_3_) | copy-start | bytes 786436
  15.9 12.2 %copy-start.13 = (f32[3,128,512]{2,1,0:T(8,128)}, f32[3,128,512]{2,1,0:T(8,128)S(1)}, u32[]{:S(2)}) copy-start(f32[3,128,512]{2,1,0:T(8,128)S(1)} %get-tuple-element.30.refs_7_.own_a) | copy-start | bytes 2359300
  15.9 12.4 %collective-permute-start.3 = (bf16[3,128,512]{2,1,0:T(8,128)(2,1)S(1)}, bf16[3,128,512]{2,1,0:T(8,128)(2,1)S(1)}, u32[]{:S(2)}, u32[]{:S(2)}) collective-permute-start(bf16[3,128,512]{2,1,0:T(8,128)(2,1)S(1)} %get-tuple-element.33), channel_id=1, source_target_pairs={{0,1},{1,0},{2,3},{3,2},{4,5},{5,4},{6,7},{7,6},{8,9},{9,8},{10,11... | collective-permute-start | bytes 1179656 | tf_op jit(solution)/shard_map/ppermute | solution.py:263
  18.9 27.2 %copy-start.12 = (bf16[64,2048]{1,0:T(8,128)(2,1)S(1)}, bf16[64,2048]{1,0:T(8,128)(2,1)}, u32[]{:S(2)}) copy-start(bf16[64,2048]{1,0:T(8,128)(2,1)} %refs_2_.10) | copy-start | bytes 786436
  28.1 15.3 %copy-start.2 = (f32[3,128,1280]{2,1,0:T(8,128)}, f32[3,128,1280]{2,1,0:T(8,128)S(1)}, u32[]{:S(2)}) copy-start(f32[3,128,1280]{2,1,0:T(8,128)S(1)} %get-tuple-element.31.refs_0_.own_a) | copy-start | bytes 5898244
  28.2 23.7 %collective-permute-start.2 = (bf16[3,128,1280]{2,1,0:T(8,128)(2,1)}, bf16[3,128,1280]{2,1,0:T(8,128)(2,1)S(1)}, u32[]{:S(2)}, u32[]{:S(2)}) collective-permute-start(bf16[3,128,1280]{2,1,0:T(8,128)(2,1)} %get-tuple-element.32), channel_id=1, source_target_pairs={{0,1},{1,0},{2,3},{3,2},{4,5},{5,4},{6,7},{7,6},{8,9},{9,8},{10,11... | collective-permute-start | bytes 2949128 | tf_op jit(solution)/shard_map/ppermute | solution.py:263
  43.5 2.6 %collective-permute-start.4 = (bf16[192,2048]{1,0:T(8,128)(2,1)}, bf16[192,2048]{1,0:T(8,128)(2,1)}, u32[]{:S(2)}, u32[]{:S(2)}) collective-permute-start(bf16[192,2048]{1,0:T(8,128)(2,1)} %shard_map.78.refs_0_), channel_id=1, source_target_pairs={{0,2},{2,0},{4,6},{6,4},{8,10},{10,8},{12,14},{14,12},{1,3},{3,1},... | collective-permute-start | bytes 2359304 | tf_op jit(solution)/shard_map/ppermute | solution.py:266
  56.2 18.8 %collective-permute-start.5 = (bf16[2,384,512]{2,1,0:T(8,128)(2,1)}, bf16[2,384,512]{2,1,0:T(8,128)(2,1)}, u32[]{:S(2)}, u32[]{:S(2)}) collective-permute-start(bf16[2,384,512]{2,1,0:T(8,128)(2,1)} %get-tuple-element.37), channel_id=1, source_target_pairs={{0,1},{1,0},{2,3},{3,2},{4,5},{5,4},{6,7},{7,6},{8,9},{9,8},{10,11... | collective-permute-start | bytes 2359304 | tf_op jit(solution)/shard_map/ppermute | solution.py:263
  56.8 23.5 %copy-start.10 = (bf16[64,2048]{1,0:T(8,128)(2,1)S(1)}, bf16[64,2048]{1,0:T(8,128)(2,1)}, u32[]{:S(2)}) copy-start(bf16[64,2048]{1,0:T(8,128)(2,1)} %refs_2_.13) | copy-start | bytes 786436
  77.9 2.4 %collective-permute-start.6 = (bf16[192,2048]{1,0:T(8,128)(2,1)S(1)}, bf16[192,2048]{1,0:T(8,128)(2,1)S(1)}, u32[]{:S(2)}, u32[]{:S(2)}) collective-permute-start(bf16[192,2048]{1,0:T(8,128)(2,1)S(1)} %shard_map.82.refs_0_), channel_id=1, source_target_pairs={{0,2},{2,0},{4,6},{6,4},{8,10},{10,8},{12,14},{14,12},{1,3},{3,1},... | collective-permute-start | bytes 2359304 | tf_op jit(solution)/shard_map/ppermute | solution.py:266
  78.0 20.6 %collective-permute-start.7 = (bf16[2,384,512]{2,1,0:T(8,128)(2,1)}, bf16[2,384,512]{2,1,0:T(8,128)(2,1)S(1)}, u32[]{:S(2)}, u32[]{:S(2)}) collective-permute-start(bf16[2,384,512]{2,1,0:T(8,128)(2,1)} %copy-done.28), channel_id=1, source_target_pairs={{0,1},{1,0},{2,3},{3,2},{4,5},{5,4},{6,7},{7,6},{8,9},{9,8},{10,11... | collective-permute-start | bytes 2359304 | tf_op jit(solution)/shard_map/ppermute | solution.py:263
  81.7 19.7 %copy-start = (bf16[512,2048]{1,0:T(8,128)(2,1)}, bf16[512,2048]{1,0:T(8,128)(2,1)S(1)}, u32[]{:S(2)}) copy-start(bf16[512,2048]{1,0:T(8,128)(2,1)S(1)} %shard_map.83.refs_0_.refs_3_.grads) | copy-start | bytes 6291460
  85.0 21.6 %collective-permute-start.8 = (bf16[1,384,512]{2,1,0:T(8,128)(2,1)S(1)}, bf16[1,384,512]{2,1,0:T(8,128)(2,1)S(1)}, u32[]{:S(2)}, u32[]{:S(2)}) collective-permute-start(bf16[1,384,512]{2,1,0:T(8,128)(2,1)S(1)} %get-tuple-element.41), channel_id=1, source_target_pairs={{0,1},{1,0},{2,3},{3,2},{4,5},{5,4},{6,7},{7,6},{8,9},{9,8},{10,11... | collective-permute-start | bytes 1179656 | tf_op jit(solution)/shard_map/ppermute | solution.py:263
  98.6 14.8 %copy-start.15 = (bf16[2,384,512]{2,1,0:T(8,128)(2,1)}, bf16[2,384,512]{2,1,0:T(8,128)(2,1)S(1)}, u32[]{:S(2)}) copy-start(bf16[2,384,512]{2,1,0:T(8,128)(2,1)S(1)} %collective-permute-done.7.refs_3_.got_t) | copy-start | bytes 2359300
  101.5 12.0 %copy-start.17 = (f32[1,384,512]{2,1,0:T(8,128)}, f32[1,384,512]{2,1,0:T(8,128)S(1)}, u32[]{:S(2)}) copy-start(f32[1,384,512]{2,1,0:T(8,128)S(1)} %get-tuple-element.40.refs_5_.own_g) | copy-start | bytes 2359300
  113.4 56.1 %collective-permute-start.11 = (bf16[3,384,512]{2,1,0:T(8,128)(2,1)}, bf16[3,384,512]{2,1,0:T(8,128)(2,1)}, u32[]{:S(2)}, u32[]{:S(2)}) collective-permute-start(bf16[3,384,512]{2,1,0:T(8,128)(2,1)} %get-tuple-element.47), channel_id=1, source_target_pairs={{0,1},{1,0},{2,3},{3,2},{4,5},{5,4},{6,7},{7,6},{8,9},{9,8},{10,11... | collective-permute-start | bytes 3538952 | tf_op jit(solution)/shard_map/ppermute | solution.py:263
  114.3 35.4 %collective-permute-start.9 = (bf16[1,384,512]{2,1,0:T(8,128)(2,1)S(1)}, bf16[1,384,512]{2,1,0:T(8,128)(2,1)S(1)}, u32[]{:S(2)}, u32[]{:S(2)}) collective-permute-start(bf16[1,384,512]{2,1,0:T(8,128)(2,1)S(1)} %get-tuple-element.43), channel_id=1, source_target_pairs={{0,1},{1,0},{2,3},{3,2},{4,5},{5,4},{6,7},{7,6},{8,9},{9,8},{10,11... | collective-permute-start | bytes 1179656 | tf_op jit(solution)/shard_map/ppermute | solution.py:263
  153.6 8.4 %copy-start.16 = (bf16[2,384,512]{2,1,0:T(8,128)(2,1)S(1)}, bf16[2,384,512]{2,1,0:T(8,128)(2,1)}, u32[]{:S(2)}) copy-start(bf16[2,384,512]{2,1,0:T(8,128)(2,1)} %copy-done.15) | copy-start | bytes 2359300
  153.6 8.4 %copy-start.18 = (f32[1,384,512]{2,1,0:T(8,128)S(1)}, f32[1,384,512]{2,1,0:T(8,128)}, u32[]{:S(2)}) copy-start(f32[1,384,512]{2,1,0:T(8,128)} %copy-done.17) | copy-start | bytes 2359300
  153.6 24.1 %collective-permute-start.10 = (bf16[3,384,256]{2,1,0:T(8,128)(2,1)S(1)}, bf16[3,384,256]{2,1,0:T(8,128)(2,1)S(1)}, u32[]{:S(2)}, u32[]{:S(2)}) collective-permute-start(bf16[3,384,256]{2,1,0:T(8,128)(2,1)S(1)} %get-tuple-element.45), channel_id=1, source_target_pairs={{0,1},{1,0},{2,3},{3,2},{4,5},{5,4},{6,7},{7,6},{8,9},{9,8},{10,11... | collective-permute-start | bytes 1769480 | tf_op jit(solution)/shard_map/ppermute | solution.py:263
  (19 other events, 53.3 us)
Sparse Core Ops, SparseCore 0:
  9.6 30.6 all-gather.2
  43.6 27.5 all-gather.4

commit v3 on v2

--- a/solution.py
+++ b/solution.py
@@ -275,7 +275,7 @@
     near_grad = [out_grad, sibling(out_grad)]
     token_blocks, grad_blocks = gather(tokens), gather(out_grad)
     near = (n_own, n_own)
-    far = ((n_feat - 2) * n_own,)
+    far = ((n_feat // 2 - 1) * n_own,) * 2
 
     def near_part(first, width, after):
         own, send = partial(
@@ -285,8 +285,8 @@
 
     def far_part(first, width, kinds, after):
         own, send = partial(
-            [all_tokens] if "t" in kinds else None,
-            [all_grad] if "g" in kinds else None,
+            far_tokens if "t" in kinds else None,
+            far_grad if "g" in kinds else None,
             far,
             weights if "t" in kinds else (),
             down_weight if "g" in kinds else None,
@@ -294,28 +294,29 @@
         )
         return own, swap(send)
 
-    def joined(blocks, near_pieces, flip, after):
+    def far_rows(blocks, after):
         mine = others(blocks, n_own, after)
-        return join([mine, sibling(mine)] + near_pieces, flip, ())
+        return [mine, sibling(mine)]
 
     a0 = near_part(0, wide, ())
     a1 = near_part(wide, hidden_units - wide, (a0[0],))
-    all_tokens, flipped = joined(token_blocks, near_tokens, True, (a1[0], a0[1]))
-    t0 = far_part(0, wide, "t", (a1[1],))
-    t1 = far_part(wide, wide, "t", (t0[0],))
-    all_grad = joined(grad_blocks, near_grad, False, (t1[0], t0[1]))[0]
-    g0 = far_part(0, wide, "g", (t1[0],))
-    g1 = far_part(wide, wide, "g", (g0[0], t1[1]))
-    f2 = far_part(2 * wide, wide, "tg", (g1[0], g0[1]))
-    f3 = far_part(3 * wide, hidden_units - 3 * wide, "tg", (f2[0], g1[1]))
+    far_tokens = far_rows(token_blocks, (a1[0], a0[1]))
+    t01 = far_part(0, 2 * wide, "t", (a1[1],))
+    flipped = join(far_tokens + near_tokens, True, (t01[0],))[1]
+    far_grad = far_rows(grad_blocks, (t01[0],))
+    g01 = far_part(0, 2 * wide, "g", (t01[0],))
+    all_grad = join(far_grad + near_grad, False, (g01[0],))[0]
+    f2 = far_part(2 * wide, wide, "tg", (g01[0], t01[1]))
+    f3 = far_part(3 * wide, hidden_units - 3 * wide, "tg", (f2[0], g01[1]))
 
     outs = None
-    for first, width, a, a_first, t, g, far_first, after in (
-        (0, wide, a0, 0, t0, g0, 0, (f2[0],)),
-        (wide, wide, a1, 0, t1, g1, 0, (f3[0],)),
-        (2 * wide, wide, a1, wide, f2, f2, 0, ()),
-        (3 * wide, hidden_units - 3 * wide, a1, 2 * wide, f3, f3, 0, ()),
+    for first, width, a, a_first, t, g, after in (
+        (0, wide, a0, 0, t01, g01, (f3[0],)),
+        (wide, wide, a1, 0, t01, g01, ()),
+        (2 * wide, wide, a1, wide, f2, f2, ()),
+        (3 * wide, hidden_units - 3 * wide, a1, 2 * wide, f3, f3, ()),
     ):
+        far_first = wide if first == wide else 0
         outs = group_grads(
             first, width, a, a_first, t, g, far_first, flipped, all_grad, hidden_units,
             outs, after,

time: 191 us -> 163 us (0.85)
  waiting for transfers between devices: 82.5 us -> 62.8 us
  local copies, waits for them, and re-layouts: 12.8 us -> 9.57 us
  starting transfers between devices: 9.09 us -> 6.66 us
  Pallas kernels: 71.4 us -> 69.4 us
    ppermute x8 -> x6, waiting for transfers between devices: 57.7 us -> 37 us  [swap(): return lax.ppermute(x, 'tok', [(0, 1), (1, 0)])]
    unnamed x58 -> x50, local copies, waits for them, and re-layouts: 12.8 us -> 9.57 us
    all_gather x2, waiting for transfers between devices: 18.5 us -> 21.1 us  [gather(): lax.all_gather(x, 'feat', axis=0, tiled=True, axis_index_groups=[list(ran...]
    pallas_call x8 -> x6, Pallas kernels: 38.1 us -> 35.5 us  [partial_products(): pl.pallas_call(functools.partial(partial_kernel, len(heights), n_token, n...]
    ppermute x8 -> x6, starting transfers between devices: 8.34 us -> 5.92 us  [swap(): return lax.ppermute(x, 'tok', [(0, 1), (1, 0)])]
  transfers between devices with their start and end apart: 14 -> 12, of which waited for: 11 -> 9; matrix products, arithmetic and copies ran while one was open for 0% -> 0% of each run, Pallas kernels for 31% -> 39%
where the time goes in v3:
time: 163 us
  Pallas kernels  69.4 us (43%)
  waiting for transfers between devices  62.8 us (39%)
  between operations  14.2 us (9%)
  local copies, waits for them, and re-layouts  9.57 us (6%)
  starting transfers between devices  6.66 us (4%)
    ppermute x6, waiting for transfers between devices, swap(): return lax.ppermute(x, 'tok', [(0, 1), (1, 0)])  37 us
    pallas_call x6, Pallas kernels, partial_products(): pl.pallas_call(functools.partial(partial_kernel, len(heights), n_token, n...  35.5 us
    pallas_call x4, Pallas kernels, group_grads(): pl.pallas_call(grads_kernel, grid=(steps,), in_specs=specs, out_specs=[pl...  30.5 us
    all_gather x2, waiting for transfers between devices, gather(): lax.all_gather(x, 'feat', axis=0, tiled=True, axis_index_groups=[list(ran...  21.1 us
    unnamed x50, local copies, waits for them, and re-layouts  9.57 us
    ppermute x6, starting transfers between devices, swap(): return lax.ppermute(x, 'tok', [(0, 1), (1, 0)])  5.92 us
    ppermute x4, waiting for transfers between devices, sibling(): return lax.ppermute(x, 'feat', [(i, i ^ 1) for i in range(n_feat)])  3.94 us
  transfers between devices with their start and end apart: 12, of which 9 were waited for; matrix products, arithmetic and copies ran while one was open for 0% of the time, Pallas kernels for 39%

profile of v3, /device:TPU:0, one launch (start us, length us, event | category | flops | bytes accessed | tf_op | source)
XLA Modules:
  0.0 162.7 jit_solution(7224522464431920973)
XLA Ops:
  8.5 1.3 collective-permute-done.refs_1_.refs_3_
  12.1 3.8 %shard_map.76 = (f32[3,128,512]{2,1,0:T(8,128)S(1)}, bf16[3,128,512]{2,1,0:T(8,128)(2,1)S(1)}) custom-call(bf16[64,2048]{1,0:T(8,128)(2,1)S(1)} %copy-done.11, bf16[64,2048]{1,0:T(8,128)(2,1)S(1)} %collective-permute-done.refs_1_.refs_3_, bf16[2048,1792]{1,0:T(8,128)(2,1)} %refs_2_.13, bf16[2048,1792]{1,0:T(8,128)(2,1)} %refs_3_.9, ...), custom_call_target="tpu_custom_call" | custom-call | flops 1024 | bytes 1024 | tf_op jit(solution)/shard_map/pallas_call | solution.py:104
  15.9 2.9 %collective-permute-start.3 = (bf16[3,128,512]{2,1,0:T(8,128)(2,1)S(1)}, bf16[3,128,512]{2,1,0:T(8,128)(2,1)S(1)}, u32[]{:S(2)}, u32[]{:S(2)}) collective-permute-start(bf16[3,128,512]{2,1,0:T(8,128)(2,1)S(1)} %get-tuple-element.28), channel_id=1, source_target_pairs={{0,1},{1,0},{2,3},{3,2},{4,5},{5,4},{6,7},{7,6},{8,9},{9,8},{10,11... | collective-permute-start | bytes 1179656 | tf_op jit(solution)/shard_map/ppermute | solution.py:263
  18.9 9.2 %shard_map.77 = (f32[3,128,1280]{2,1,0:T(8,128)S(1)}, bf16[3,128,1280]{2,1,0:T(8,128)(2,1)}) custom-call(bf16[64,2048]{1,0:T(8,128)(2,1)S(1)} %copy-done.11, bf16[64,2048]{1,0:T(8,128)(2,1)S(1)} %collective-permute-done.refs_1_.refs_3_, bf16[2048,1792]{1,0:T(8,128)(2,1)} %refs_2_.13, bf16[2048,1792]{1,0:T(8,128)(2,1)} %refs_3_.9, ...), custom_call_target="tpu_custom_call" | custom-call | flops 1024 | bytes 1024 | tf_op jit(solution)/shard_map/pallas_call | solution.py:104
  28.3 12.0 %all-gather.3.cloned.1.call-done.blocks_ref = bf16[256,2048]{1,0:T(8,128)(2,1)} async-done(((bf16[64,2048]{1,0:T(8,128)(2,1)}), bf16[256,2048]{1,0:T(8,128)(2,1)}) %all-gather.3.cloned.1.call-update) | async-done | bytes 1048592 | tf_op jit(solution)/shard_map/all_gather | solution.py:269
  40.2 1.2 copy-done.24
  42.5 9.4 %collective-permute-done.2.refs_4_.got_a = bf16[3,128,1280]{2,1,0:T(8,128)(2,1)} collective-permute-done((bf16[3,128,1280]{2,1,0:T(8,128)(2,1)}, bf16[3,128,1280]{2,1,0:T(8,128)(2,1)}, u32[]{:S(2)}, u32[]{:S(2)}) %collective-permute-start.2) | collective-permute-done | bytes 983072 | tf_op jit(solution)/shard_map/ppermute | solution.py:263
  51.9 7.8 %shard_map.79 = (f32[2,384,1024]{2,1,0:T(8,128)}, bf16[2,384,1024]{2,1,0:T(8,128)(2,1)}) custom-call(bf16[192,2048]{1,0:T(8,128)(2,1)S(1)} %shard_map.78.refs_0_, bf16[192,2048]{1,0:T(8,128)(2,1)S(1)} %collective-permute-done.4.refs_1_, bf16[2048,1792]{1,0:T(8,128)(2,1)} %refs_2_.13, bf16[2048,1792]{1,0:T(8,128)(2,1)} %refs_3_.9, ...), custom_call_target="tpu_custom_call" | custom-call | flops 1024 | bytes 1024 | tf_op jit(solution)/shard_map/pallas_call | solution.py:104
  60.1 9.2 %all-gather.5.cloned.1.call-done.blocks_ref = bf16[256,2048]{1,0:T(8,128)(2,1)} async-done(((bf16[64,2048]{1,0:T(8,128)(2,1)}), bf16[256,2048]{1,0:T(8,128)(2,1)}) %all-gather.5.cloned.1.call-update) | async-done | bytes 1048592 | tf_op jit(solution)/shard_map/all_gather | solution.py:269
  69.3 1.9 %copy-done = f32[2,384,1024]{2,1,0:T(8,128)S(1)} copy-done((f32[2,384,1024]{2,1,0:T(8,128)S(1)}, f32[2,384,1024]{2,1,0:T(8,128)}, u32[]{:S(2)}) %copy-start) | copy-done | bytes 3145752
  72.7 2.3 %collective-permute-done.5.refs_1_.refs_5_ = bf16[192,2048]{1,0:T(8,128)(2,1)S(1)} collective-permute-done((bf16[192,2048]{1,0:T(8,128)(2,1)S(1)}, bf16[192,2048]{1,0:T(8,128)(2,1)S(1)}, u32[]{:S(2)}, u32[]{:S(2)}) %collective-permute-start.5) | collective-permute-done | bytes 786464 | tf_op jit(solution)/shard_map/ppermute | solution.py:266
  75.0 4.5 %shard_map.81 = (f32[1,384,1024]{2,1,0:T(8,128)S(1)}, bf16[1,384,1024]{2,1,0:T(8,128)(2,1)S(1)}) custom-call(bf16[192,2048]{1,0:T(8,128)(2,1)S(1)} %shard_map.80.refs_0_.refs_4_, bf16[192,2048]{1,0:T(8,128)(2,1)S(1)} %collective-permute-done.5.refs_1_.refs_5_, bf16[1792,2048]{1,0:T(8,128)(2,1)} %refs_6_.7, ...), custom_call_target="tpu_custom_call" | custom-call | flops 1024 | bytes 1024 | tf_op jit(solution)/shard_map/pallas_call | solution.py:104
  79.5 1.5 collective-permute-start.7
  81.0 16.2 %collective-permute-done.6.refs_8_.got_t = bf16[2,384,1024]{2,1,0:T(8,128)(2,1)S(1)} collective-permute-done((bf16[2,384,1024]{2,1,0:T(8,128)(2,1)}, bf16[2,384,1024]{2,1,0:T(8,128)(2,1)S(1)}, u32[]{:S(2)}, u32[]{:S(2)}) %collective-permute-start.6) | collective-permute-done | bytes 1572896 | tf_op jit(solution)/shard_map/ppermute | solution.py:263
  98.4 6.1 %shard_map.82 = (f32[3,384,512]{2,1,0:T(8,128)}, bf16[3,384,512]{2,1,0:T(8,128)(2,1)}) custom-call(bf16[192,2048]{1,0:T(8,128)(2,1)S(1)} %shard_map.78.refs_0_, bf16[192,2048]{1,0:T(8,128)(2,1)S(1)} %collective-permute-done.4.refs_1_, bf16[2048,1792]{1,0:T(8,128)(2,1)} %refs_2_.13, bf16[2048,1792]{1,0:T(8,128)(2,1)} %refs_3_.9, ...), custom_call_target="tpu_custom_call" | custom-call | flops 1024 | bytes 1024 | tf_op jit(solution)/shard_map/pallas_call | solution.py:104
  104.8 9.2 %collective-permute-done.7.refs_8_.got_g = bf16[1,384,1024]{2,1,0:T(8,128)(2,1)S(1)} collective-permute-done((bf16[1,384,1024]{2,1,0:T(8,128)(2,1)S(1)}, bf16[1,384,1024]{2,1,0:T(8,128)(2,1)S(1)}, u32[]{:S(2)}, u32[]{:S(2)}) %collective-permute-start.7) | collective-permute-done | bytes 786464 | tf_op jit(solution)/shard_map/ppermute | solution.py:263
  114.1 4.2 %shard_map.83 = (f32[3,384,256]{2,1,0:T(8,128)S(1)}, bf16[3,384,256]{2,1,0:T(8,128)(2,1)}) custom-call(bf16[192,2048]{1,0:T(8,128)(2,1)S(1)} %shard_map.78.refs_0_, bf16[192,2048]{1,0:T(8,128)(2,1)S(1)} %collective-permute-done.4.refs_1_, bf16[2048,1792]{1,0:T(8,128)(2,1)} %refs_2_.13, bf16[2048,1792]{1,0:T(8,128)(2,1)} %refs_3_.9, ...), custom_call_target="tpu_custom_call" | custom-call | flops 1024 | bytes 1024 | tf_op jit(solution)/shard_map/pallas_call | solution.py:104
  118.8 2.4 %shard_map.84 = (bf16[512,2048]{1,0:T(8,128)(2,1)}, bf16[2048,512]{1,0:T(8,128)(2,1)}) custom-call(bf16[192,2048]{1,0:T(8,128)(2,1)S(1)} %shard_map.78.refs_0_, bf16[192,2048]{1,0:T(8,128)(2,1)S(1)} %collective-permute-done.4.refs_1_, bf16[64,2048]{1,0:T(8,128)(2,1)S(1)} %copy-done.12, bf16[64,2048]{1,0:T(8,128)(2,1)S(1)} %copy-done.20, ...), custom_call_target="tpu_custom_call" | custom-call | flops 1024 | bytes 1024 | tf_op jit(solution)/shard_map/pallas_call | solution.py:135
  121.7 1.4 copy-done.1
  123.1 8.0 %shard_map.86 = (bf16[2048,1792]{1,0:T(8,128)(2,1)}, bf16[2048,1792]{1,0:T(8,128)(2,1)}, bf16[1792,2048]{1,0:T(8,128)(2,1)}) custom-call(f32[3,128,512]{2,1,0:T(8,128)S(1)} %copy-done.16, bf16[3,128,512]{2,1,0:T(8,128)(2,1)S(1)} %copy-done.22, f32[2,384,1024]{2,1,0:T(8,128)} %get-tuple-element.29.refs_0_.refs_3_.refs_4_.own_t, ...), custom_call_target="tpu_custom_call" | custom-call | flops 1024 | bytes 1024 | tf_op jit(solution)/shard_map/pallas_call | solution.py:234
  131.1 8.4 %shard_map.87 = (bf16[2048,1792]{1,0:T(8,128)(2,1)}, bf16[2048,1792]{1,0:T(8,128)(2,1)}, bf16[1792,2048]{1,0:T(8,128)(2,1)}) custom-call(f32[3,128,1280]{2,1,0:T(8,128)} %copy-done.3, bf16[3,128,1280]{2,1,0:T(8,128)(2,1)} %collective-permute-done.2.refs_4_.got_a, ...), custom_call_target="tpu_custom_call", output_to_operand_aliasing={{0}: (8, {}), {1}: (9, {}), {2}: (10, {})} | custom-call | flops 1024 | bytes 1024 | tf_op jit(solution)/shard_map/pallas_call | solution.py:234
  139.6 8.3 %shard_map.88 = (bf16[2048,1792]{1,0:T(8,128)(2,1)}, bf16[2048,1792]{1,0:T(8,128)(2,1)}, bf16[1792,2048]{1,0:T(8,128)(2,1)}) custom-call(f32[3,128,1280]{2,1,0:T(8,128)S(1)} %copy-done.4, bf16[3,128,1280]{2,1,0:T(8,128)(2,1)} %collective-permute-done.2.refs_4_.got_a, ...), custom_call_target="tpu_custom_call", output_to_operand_aliasing={{0}: (8, {}), {1}: (9, {}), {2}: (10, {})} | custom-call | flops 1024 | bytes 1024 | tf_op jit(solution)/shard_map/pallas_call | solution.py:234
  147.8 2.2 %collective-permute-done.8.got_t.got_g = bf16[3,384,256]{2,1,0:T(8,128)(2,1)} collective-permute-done((bf16[3,384,256]{2,1,0:T(8,128)(2,1)}, bf16[3,384,256]{2,1,0:T(8,128)(2,1)}, u32[]{:S(2)}, u32[]{:S(2)}) %collective-permute-start.8) | collective-permute-done | bytes 589856 | tf_op jit(solution)/shard_map/ppermute | solution.py:263
  150.0 5.8 %shard_map.89 = (bf16[2048,1792]{1,0:T(8,128)(2,1)}, bf16[2048,1792]{1,0:T(8,128)(2,1)}, bf16[1792,2048]{1,0:T(8,128)(2,1)}) custom-call(f32[3,128,1280]{2,1,0:T(8,128)S(1)} %copy-done.4, bf16[3,128,1280]{2,1,0:T(8,128)(2,1)} %collective-permute-done.2.refs_4_.got_a, ...), custom_call_target="tpu_custom_call", output_to_operand_aliasing={{0}: (8, {}), {1}: (9, {}), {2}: (10, {})} | custom-call | flops 1024 | bytes 1024 | tf_op jit(solution)/shard_map/pallas_call | solution.py:234
  (66 shorter events, 9.4 us)
Async XLA Ops:
  7.2 33.1 %all-gather.3.cloned.1.call-start = ((), (), s32[]{:S(2)}) async-start(), calls=%async_computation | async-start | bytes 1310720 | tf_op jit(solution)/shard_map/all_gather | solution.py:269
  7.9 61.4 %all-gather.5.cloned.1.call-start = ((), (), s32[]{:S(2)}) async-start(), calls=%async_computation.1 | async-start | bytes 1310720 | tf_op jit(solution)/shard_map/all_gather | solution.py:269
  7.9 1.9 %collective-permute-start = (bf16[64,2048]{1,0:T(8,128)(2,1)}, bf16[64,2048]{1,0:T(8,128)(2,1)S(1)}, u32[]{:S(2)}, u32[]{:S(2)}) collective-permute-start(bf16[64,2048]{1,0:T(8,128)(2,1)} %refs_2_.14), channel_id=1, source_target_pairs={{0,2},{2,0},{4,6},{6,4},{8,10},{10,8},{12,14},{14,12},{1,3},{3,1},... | collective-permute-start | bytes 786440 | tf_op jit(solution)/shard_map/ppermute | solution.py:266
  8.5 1.7 %collective-permute-start.1 = (bf16[64,2048]{1,0:T(8,128)(2,1)}, bf16[64,2048]{1,0:T(8,128)(2,1)S(1)}, u32[]{:S(2)}, u32[]{:S(2)}) collective-permute-start(bf16[64,2048]{1,0:T(8,128)(2,1)} %refs_2_.15), channel_id=1, source_target_pairs={{0,2},{2,0},{4,6},{6,4},{8,10},{10,8},{12,14},{14,12},{1,3},{3,1},... | collective-permute-start | bytes 786440 | tf_op jit(solution)/shard_map/ppermute | solution.py:266
  9.8 9.0 %copy-start.19 = (bf16[64,2048]{1,0:T(8,128)(2,1)}, bf16[64,2048]{1,0:T(8,128)(2,1)S(1)}, u32[]{:S(2)}) copy-start(bf16[64,2048]{1,0:T(8,128)(2,1)S(1)} %collective-permute-done.refs_1_.refs_3_) | copy-start | bytes 786436
  12.1 6.8 %copy-start.17 = (bf16[64,2048]{1,0:T(8,128)(2,1)}, bf16[64,2048]{1,0:T(8,128)(2,1)S(1)}, u32[]{:S(2)}) copy-start(bf16[64,2048]{1,0:T(8,128)(2,1)S(1)} %collective-permute-done.1.refs_5_.refs_3_) | copy-start | bytes 786436
  15.9 12.2 %copy-start.15 = (f32[3,128,512]{2,1,0:T(8,128)}, f32[3,128,512]{2,1,0:T(8,128)S(1)}, u32[]{:S(2)}) copy-start(f32[3,128,512]{2,1,0:T(8,128)S(1)} %get-tuple-element.25.refs_7_.own_a) | copy-start | bytes 2359300
  15.9 12.3 %collective-permute-start.3 = (bf16[3,128,512]{2,1,0:T(8,128)(2,1)S(1)}, bf16[3,128,512]{2,1,0:T(8,128)(2,1)S(1)}, u32[]{:S(2)}, u32[]{:S(2)}) collective-permute-start(bf16[3,128,512]{2,1,0:T(8,128)(2,1)S(1)} %get-tuple-element.28), channel_id=1, source_target_pairs={{0,1},{1,0},{2,3},{3,2},{4,5},{5,4},{6,7},{7,6},{8,9},{9,8},{10,11... | collective-permute-start | bytes 1179656 | tf_op jit(solution)/shard_map/ppermute | solution.py:263
  28.1 31.6 %copy-start.3 = (f32[3,128,1280]{2,1,0:T(8,128)}, f32[3,128,1280]{2,1,0:T(8,128)S(1)}, u32[]{:S(2)}) copy-start(f32[3,128,1280]{2,1,0:T(8,128)S(1)} %get-tuple-element.26.refs_0_.own_a) | copy-start | bytes 5898244
  28.1 23.8 %collective-permute-start.2 = (bf16[3,128,1280]{2,1,0:T(8,128)(2,1)}, bf16[3,128,1280]{2,1,0:T(8,128)(2,1)}, u32[]{:S(2)}, u32[]{:S(2)}) collective-permute-start(bf16[3,128,1280]{2,1,0:T(8,128)(2,1)} %get-tuple-element.27), channel_id=1, source_target_pairs={{0,1},{1,0},{2,3},{3,2},{4,5},{5,4},{6,7},{7,6},{8,9},{9,8},{10,11... | collective-permute-start | bytes 2949128 | tf_op jit(solution)/shard_map/ppermute | solution.py:263
  42.5 9.4 %collective-permute-start.4 = (bf16[192,2048]{1,0:T(8,128)(2,1)S(1)}, bf16[192,2048]{1,0:T(8,128)(2,1)S(1)}, u32[]{:S(2)}, u32[]{:S(2)}) collective-permute-start(bf16[192,2048]{1,0:T(8,128)(2,1)S(1)} %shard_map.78.refs_0_), channel_id=1, source_target_pairs={{0,2},{2,0},{4,6},{6,4},{8,10},{10,8},{12,14},{14,12},{1,3},{3,1},... | collective-permute-start | bytes 2359304 | tf_op jit(solution)/shard_map/ppermute | solution.py:266
  59.7 37.5 %collective-permute-start.6 = (bf16[2,384,1024]{2,1,0:T(8,128)(2,1)}, bf16[2,384,1024]{2,1,0:T(8,128)(2,1)S(1)}, u32[]{:S(2)}, u32[]{:S(2)}) collective-permute-start(bf16[2,384,1024]{2,1,0:T(8,128)(2,1)} %get-tuple-element.31), channel_id=1, source_target_pairs={{0,1},{1,0},{2,3},{3,2},{4,5},{5,4},{6,7},{7,6},{8,9},{9,8},{10,11... | collective-permute-start | bytes 4718600 | tf_op jit(solution)/shard_map/ppermute | solution.py:263
  72.6 2.4 %collective-permute-start.5 = (bf16[192,2048]{1,0:T(8,128)(2,1)S(1)}, bf16[192,2048]{1,0:T(8,128)(2,1)S(1)}, u32[]{:S(2)}, u32[]{:S(2)}) collective-permute-start(bf16[192,2048]{1,0:T(8,128)(2,1)S(1)} %shard_map.80.refs_0_.refs_4_), channel_id=1, source_target_pairs={{0,2},{2,0},{4,6},{6,4},{8,10},{10,8},{12,14},{14,12},{1,3},{3,1},... | collective-permute-start | bytes 2359304 | tf_op jit(solution)/shard_map/ppermute | solution.py:266
  79.5 41.7 %copy-start.5 = (f32[1,384,1024]{2,1,0:T(8,128)}, f32[1,384,1024]{2,1,0:T(8,128)S(1)}, u32[]{:S(2)}) copy-start(f32[1,384,1024]{2,1,0:T(8,128)S(1)} %get-tuple-element.30.refs_7_.refs_4_.own_g) | copy-start | bytes 4718596
  79.5 34.6 %collective-permute-start.7 = (bf16[1,384,1024]{2,1,0:T(8,128)(2,1)S(1)}, bf16[1,384,1024]{2,1,0:T(8,128)(2,1)S(1)}, u32[]{:S(2)}, u32[]{:S(2)}) collective-permute-start(bf16[1,384,1024]{2,1,0:T(8,128)(2,1)S(1)} %get-tuple-element.33), channel_id=1, source_target_pairs={{0,1},{1,0},{2,3},{3,2},{4,5},{5,4},{6,7},{7,6},{8,9},{9,8},{10,11... | collective-permute-start | bytes 2359304 | tf_op jit(solution)/shard_map/ppermute | solution.py:263
  104.4 35.1 %collective-permute-start.9 = (bf16[3,384,512]{2,1,0:T(8,128)(2,1)}, bf16[3,384,512]{2,1,0:T(8,128)(2,1)}, u32[]{:S(2)}, u32[]{:S(2)}) collective-permute-start(bf16[3,384,512]{2,1,0:T(8,128)(2,1)} %get-tuple-element.37), channel_id=1, source_target_pairs={{0,1},{1,0},{2,3},{3,2},{4,5},{5,4},{6,7},{7,6},{8,9},{9,8},{10,11... | collective-permute-start | bytes 3538952 | tf_op jit(solution)/shard_map/ppermute | solution.py:263
  114.1 7.1 %copy-start.14 = (bf16[64,2048]{1,0:T(8,128)(2,1)S(1)}, bf16[64,2048]{1,0:T(8,128)(2,1)}, u32[]{:S(2)}) copy-start(bf16[64,2048]{1,0:T(8,128)(2,1)} %refs_2_.15) | copy-start | bytes 786436
  114.1 7.1 %copy-start.18 = (bf16[64,2048]{1,0:T(8,128)(2,1)S(1)}, bf16[64,2048]{1,0:T(8,128)(2,1)}, u32[]{:S(2)}) copy-start(bf16[64,2048]{1,0:T(8,128)(2,1)} %copy-done.17) | copy-start | bytes 786436
  118.3 12.9 %copy-start.9 = (f32[3,384,256]{2,1,0:T(8,128)}, f32[3,384,256]{2,1,0:T(8,128)S(1)}, u32[]{:S(2)}) copy-start(f32[3,384,256]{2,1,0:T(8,128)S(1)} %get-tuple-element.34.rest_0_.own_t.own_g) | copy-start | bytes 3538948
  118.3 31.8 %collective-permute-start.8 = (bf16[3,384,256]{2,1,0:T(8,128)(2,1)}, bf16[3,384,256]{2,1,0:T(8,128)(2,1)}, u32[]{:S(2)}, u32[]{:S(2)}) collective-permute-start(bf16[3,384,256]{2,1,0:T(8,128)(2,1)} %get-tuple-element.35), channel_id=1, source_target_pairs={{0,1},{1,0},{2,3},{3,2},{4,5},{5,4},{6,7},{7,6},{8,9},{9,8},{10,11... | collective-permute-start | bytes 1769480 | tf_op jit(solution)/shard_map/ppermute | solution.py:263
  123.1 8.1 %copy-start.6 = (f32[1,384,1024]{2,1,0:T(8,128)S(1)}, f32[1,384,1024]{2,1,0:T(8,128)}, u32[]{:S(2)}) copy-start(f32[1,384,1024]{2,1,0:T(8,128)} %copy-done.5) | copy-start | bytes 4718596
  131.1 8.4 %copy-start.2 = (bf16[2048,512]{1,0:T(8,128)(2,1)S(1)}, bf16[2048,512]{1,0:T(8,128)(2,1)}, u32[]{:S(2)}) copy-start(bf16[2048,512]{1,0:T(8,128)(2,1)} %get-tuple-element.36.flipped) | copy-start | bytes 6291460
  131.1 8.4 %copy-start.4 = (f32[3,128,1280]{2,1,0:T(8,128)S(1)}, f32[3,128,1280]{2,1,0:T(8,128)}, u32[]{:S(2)}) copy-start(f32[3,128,1280]{2,1,0:T(8,128)} %copy-done.3) | copy-start | bytes 5898244
  139.6 10.5 %copy-start.10 = (f32[3,384,256]{2,1,0:T(8,128)S(1)}, f32[3,384,256]{2,1,0:T(8,128)}, u32[]{:S(2)}) copy-start(f32[3,384,256]{2,1,0:T(8,128)} %copy-done.9) | copy-start | bytes 3538948
  (13 other events, 33.3 us)
Sparse Core Ops, SparseCore 0:
  9.6 30.6 all-gather.2
  41.8 27.4 all-gather.4

commit v4 on v3

--- a/solution.py
+++ b/solution.py
@@ -142,29 +142,6 @@
         compiler_params=pltpu.CompilerParams(vmem_limit_bytes=VMEM_LIMIT),
         cost_estimate=SMALL_COST,
     )(*pieces, *after)
-
-
-def others_kernel(n_own, blocks_ref, *refs):
-    n_chips = blocks_ref.shape[0] // n_own
-    chip = lax.axis_index("feat") // 2
-    for k in range(1, n_chips):
-        row = pl.multiple_of(lax.rem(chip + k, n_chips) * n_own, n_own)
-        refs[-1][(k - 1) * n_own : k * n_own, :] = blocks_ref[pl.ds(row, n_own), :]
-
-
-def others(blocks, n_own, after):
-    n_rows, depth = blocks.shape
-    tile = depth // 2
-    return pl.pallas_call(
-        functools.partial(others_kernel, n_own),
-        grid=(2,),
-        in_specs=[pl.BlockSpec((n_rows, tile), lambda i: (0, i))]
-        + [pl.BlockSpec(memory_space=pl.ANY)] * len(after),
-        out_specs=pl.BlockSpec((n_rows - n_own, tile), lambda i: (0, i)),
-        out_shape=jax.ShapeDtypeStruct((n_rows - n_own, depth), BF16),
-        compiler_params=pltpu.CompilerParams(vmem_limit_bytes=VMEM_LIMIT),
-        cost_estimate=SMALL_COST,
-    )(blocks, *after)
 
 
 def grads_kernel(own_a, got_a, own_t, got_t, own_g, got_g, flipped, grads, *rest):
@@ -266,10 +243,10 @@
         return lax.ppermute(x, "feat", [(i, i ^ 1) for i in range(n_feat)])
 
     def gather(x):
-        return lax.all_gather(
-            x, "feat", axis=0, tiled=True,
-            axis_index_groups=[list(range(c, n_feat, 2)) for c in range(2)],
-        )
+        return [
+            lax.ppermute(x, "feat", [(i, (i + k) % n_feat) for i in range(n_feat)])
+            for k in range(2, n_feat, 2)
+        ]
 
     near_tokens = [tokens, sibling(tokens)]
     near_grad = [out_grad, sibling(out_grad)]
@@ -295,7 +272,7 @@
         return own, swap(send)
 
     def far_rows(blocks, after):
-        mine = others(blocks, n_own, after)
+        mine = join(blocks, False, after)[0]
         return [mine, sibling(mine)]
 
     a0 = near_part(0, wide, ())

time: 163 us -> 152 us (0.933)
  between operations: 14.2 us -> 0.76 us
  starting transfers between devices: 6.66 us -> 17.1 us
  local copies, waits for them, and re-layouts: 9.57 us -> 6.36 us
  waiting for transfers between devices: 62.8 us -> 59.7 us
  Pallas kernels: 69.4 us -> 67.4 us
    all_gather x2 -> x0, waiting for transfers between devices: 21.1 us -> none  [gather(): lax.all_gather(x, 'feat', axis=0, tiled=True, axis_index_groups=[list(ran...]
    ppermute x0 -> x6, waiting for transfers between devices: none -> 21.1 us  [gather(): lax.ppermute(x, 'feat', [(i, (i + k) % n_feat) for i in range(n_feat)])]
    ppermute x0 -> x6, starting transfers between devices: none -> 10.2 us  [gather(): lax.ppermute(x, 'feat', [(i, (i + k) % n_feat) for i in range(n_feat)])]
    unnamed x50 -> x34, local copies, waits for them, and re-layouts: 9.57 us -> 6.36 us
    ppermute x6, waiting for transfers between devices: 37 us -> 34.7 us  [swap(): return lax.ppermute(x, 'tok', [(0, 1), (1, 0)])]
    pallas_call x2 -> x4, Pallas kernels: 2.9 us -> 3.33 us  [join(): pl.pallas_call(functools.partial(join_kernel, len(pieces), len(after)), g...]
  transfers between devices with their start and end apart: 12 -> 16, of which waited for: 9 -> 12; matrix products, arithmetic and copies ran while one was open for 0% -> 0% of each run, Pallas kernels for 39% -> 33%
where the time goes in v4:
time: 152 us; the launch traced here: 151 us
  Pallas kernels  67.4 us (44%)
  waiting for transfers between devices  59.7 us (39%)
  starting transfers between devices  17.1 us (11%)
  local copies, waits for them, and re-layouts  6.36 us (4%)
    ppermute x6, waiting for transfers between devices, swap(): return lax.ppermute(x, 'tok', [(0, 1), (1, 0)])  34.7 us
    pallas_call x6, Pallas kernels, partial_products(): pl.pallas_call(functools.partial(partial_kernel, len(heights), n_token, n...  34.1 us
    pallas_call x4, Pallas kernels, group_grads(): pl.pallas_call(grads_kernel, grid=(steps,), in_specs=specs, out_specs=[pl...  29.9 us
    ppermute x6, waiting for transfers between devices, gather(): lax.ppermute(x, 'feat', [(i, (i + k) % n_feat) for i in range(n_feat)])  21.1 us
    ppermute x6, starting transfers between devices, gather(): lax.ppermute(x, 'feat', [(i, (i + k) % n_feat) for i in range(n_feat)])  10.2 us
    unnamed x34, local copies, waits for them, and re-layouts  6.36 us
    ppermute x6, starting transfers between devices, swap(): return lax.ppermute(x, 'tok', [(0, 1), (1, 0)])  6.14 us
    ppermute x4, waiting for transfers between devices, sibling(): return lax.ppermute(x, 'feat', [(i, i ^ 1) for i in range(n_feat)])  3.94 us
  transfers between devices with their start and end apart: 16, of which 12 were waited for; matrix products, arithmetic and copies ran while one was open for 0% of the time, Pallas kernels for 33%

profile of v4, /device:TPU:0, one launch (start us, length us, event | category | flops | bytes accessed | tf_op | source)
XLA Modules:
  0.0 151.4 jit_solution(17719321247080800425)
XLA Ops:
  4.8 3.7 %shard_map.76 = (f32[3,128,512]{2,1,0:T(8,128)S(1)}, bf16[3,128,512]{2,1,0:T(8,128)(2,1)S(1)}) custom-call(bf16[64,2048]{1,0:T(8,128)(2,1)S(1)} %copy-done.9, bf16[64,2048]{1,0:T(8,128)(2,1)S(1)} %collective-permute-done.refs_1_.refs_3_, bf16[2048,1792]{1,0:T(8,128)(2,1)} %refs_2_.13, bf16[2048,1792]{1,0:T(8,128)(2,1)} %refs_3_.9, ...), custom_call_target="tpu_custom_call" | custom-call | flops 1024 | bytes 1024 | tf_op jit(solution)/shard_map/pallas_call | solution.py:104
  8.5 2.9 %collective-permute-start.6 = (bf16[3,128,512]{2,1,0:T(8,128)(2,1)S(1)}, bf16[3,128,512]{2,1,0:T(8,128)(2,1)S(1)}, u32[]{:S(2)}, u32[]{:S(2)}) collective-permute-start(bf16[3,128,512]{2,1,0:T(8,128)(2,1)S(1)} %get-tuple-element.28), channel_id=1, source_target_pairs={{0,1},{1,0},{2,3},{3,2},{4,5},{5,4},{6,7},{7,6},{8,9},{9,8},{10,11... | collective-permute-start | bytes 1179656 | tf_op jit(solution)/shard_map/ppermute | solution.py:240
  11.4 2.6 %collective-permute-start.4 = (bf16[64,2048]{1,0:T(8,128)(2,1)S(1)}, bf16[64,2048]{1,0:T(8,128)(2,1)S(1)}, u32[]{:S(2)}, u32[]{:S(2)}) collective-permute-start(bf16[64,2048]{1,0:T(8,128)(2,1)S(1)} %copy-done.9), channel_id=1, source_target_pairs={{0,8},{2,10},{4,12},{6,14},{8,0},{10,2},{12,4},{14,6},{1,9},{3,11}... | collective-permute-start | bytes 786440 | tf_op jit(solution)/shard_map/ppermute | solution.py:247
  14.0 1.6 %collective-permute-start.3 = (bf16[64,2048]{1,0:T(8,128)(2,1)S(1)}, bf16[64,2048]{1,0:T(8,128)(2,1)S(1)}, u32[]{:S(2)}, u32[]{:S(2)}) collective-permute-start(bf16[64,2048]{1,0:T(8,128)(2,1)S(1)} %copy-done.9), channel_id=1, source_target_pairs={{0,4},{2,6},{4,8},{6,10},{8,12},{10,14},{12,0},{14,2},{1,5},{3,7},... | collective-permute-start | bytes 786440 | tf_op jit(solution)/shard_map/ppermute | solution.py:247
  15.6 2.2 %collective-permute-start.5 = (bf16[64,2048]{1,0:T(8,128)(2,1)S(1)}, bf16[64,2048]{1,0:T(8,128)(2,1)S(1)}, u32[]{:S(2)}, u32[]{:S(2)}) collective-permute-start(bf16[64,2048]{1,0:T(8,128)(2,1)S(1)} %copy-done.9), channel_id=1, source_target_pairs={{0,12},{2,14},{4,0},{6,2},{8,4},{10,6},{12,8},{14,10},{1,13},{3,15... | collective-permute-start | bytes 786440 | tf_op jit(solution)/shard_map/ppermute | solution.py:247
  17.9 8.3 %shard_map.77 = (f32[3,128,1280]{2,1,0:T(8,128)S(1)}, bf16[3,128,1280]{2,1,0:T(8,128)(2,1)S(1)}) custom-call(bf16[64,2048]{1,0:T(8,128)(2,1)S(1)} %copy-done.9, bf16[64,2048]{1,0:T(8,128)(2,1)S(1)} %collective-permute-done.refs_1_.refs_3_, bf16[2048,1792]{1,0:T(8,128)(2,1)} %refs_2_.13, bf16[2048,1792]{1,0:T(8,128)(2,1)} %refs_3_.9, ...), custom_call_target="tpu_custom_call" | custom-call | flops 1024 | bytes 1024 | tf_op jit(solution)/shard_map/pallas_call | solution.py:104
  26.7 6.1 %collective-permute-done.4.refs_1_ = bf16[64,2048]{1,0:T(8,128)(2,1)S(1)} collective-permute-done((bf16[64,2048]{1,0:T(8,128)(2,1)S(1)}, bf16[64,2048]{1,0:T(8,128)(2,1)S(1)}, u32[]{:S(2)}, u32[]{:S(2)}) %collective-permute-start.4) | collective-permute-done | bytes 262176 | tf_op jit(solution)/shard_map/ppermute | solution.py:247
  33.5 15.3 %collective-permute-done.2.refs_4_.got_a = bf16[3,128,1280]{2,1,0:T(8,128)(2,1)S(1)} collective-permute-done((bf16[3,128,1280]{2,1,0:T(8,128)(2,1)S(1)}, bf16[3,128,1280]{2,1,0:T(8,128)(2,1)S(1)}, u32[]{:S(2)}, u32[]{:S(2)}) %collective-permute-start.2) | collective-permute-done | bytes 983072 | tf_op jit(solution)/shard_map/ppermute | solution.py:240
  48.9 7.5 %shard_map.79 = (f32[2,384,1024]{2,1,0:T(8,128)}, bf16[2,384,1024]{2,1,0:T(8,128)(2,1)S(1)}) custom-call(bf16[192,2048]{1,0:T(8,128)(2,1)S(1)} %shard_map.78.refs_0_, bf16[192,2048]{1,0:T(8,128)(2,1)S(1)} %collective-permute-done.7.refs_1_, bf16[2048,1792]{1,0:T(8,128)(2,1)} %refs_2_.13, bf16[2048,1792]{1,0:T(8,128)(2,1)} %refs_3_.9, ...), custom_call_target="tpu_custom_call" | custom-call | flops 1024 | bytes 1024 | tf_op jit(solution)/shard_map/pallas_call | solution.py:104
  57.8 3.0 %collective-permute-start.10 = (bf16[64,2048]{1,0:T(8,128)(2,1)S(1)}, bf16[64,2048]{1,0:T(8,128)(2,1)S(1)}, u32[]{:S(2)}, u32[]{:S(2)}) collective-permute-start(bf16[64,2048]{1,0:T(8,128)(2,1)S(1)} %copy-done.11), channel_id=1, source_target_pairs={{0,12},{2,14},{4,0},{6,2},{8,4},{10,6},{12,8},{14,10},{1,13},{3,15... | collective-permute-start | bytes 786440 | tf_op jit(solution)/shard_map/ppermute | solution.py:247
  60.8 13.7 %collective-permute-done.9.refs_1_ = bf16[64,2048]{1,0:T(8,128)(2,1)S(1)} collective-permute-done((bf16[64,2048]{1,0:T(8,128)(2,1)S(1)}, bf16[64,2048]{1,0:T(8,128)(2,1)S(1)}, u32[]{:S(2)}, u32[]{:S(2)}) %collective-permute-start.9) | collective-permute-done | bytes 262176 | tf_op jit(solution)/shard_map/ppermute | solution.py:247
  75.4 1.9 %copy-done = f32[2,384,1024]{2,1,0:T(8,128)S(1)} copy-done((f32[2,384,1024]{2,1,0:T(8,128)S(1)}, f32[2,384,1024]{2,1,0:T(8,128)}, u32[]{:S(2)}) %copy-start) | copy-done | bytes 3145752
  77.6 2.3 %collective-permute-done.11.refs_1_.refs_5_ = bf16[192,2048]{1,0:T(8,128)(2,1)S(1)} collective-permute-done((bf16[192,2048]{1,0:T(8,128)(2,1)S(1)}, bf16[192,2048]{1,0:T(8,128)(2,1)S(1)}, u32[]{:S(2)}, u32[]{:S(2)}) %collective-permute-start.11) | collective-permute-done | bytes 786464 | tf_op jit(solution)/shard_map/ppermute | solution.py:243
  79.8 4.5 %shard_map.81 = (f32[1,384,1024]{2,1,0:T(8,128)S(1)}, bf16[1,384,1024]{2,1,0:T(8,128)(2,1)S(1)}) custom-call(bf16[192,2048]{1,0:T(8,128)(2,1)S(1)} %shard_map.80.refs_0_.refs_4_, bf16[192,2048]{1,0:T(8,128)(2,1)S(1)} %collective-permute-done.11.refs_1_.refs_5_, bf16[1792,2048]{1,0:T(8,128)(2,1)} %refs_6_.7, ...), custom_call_target="tpu_custom_call" | custom-call | flops 1024 | bytes 1024 | tf_op jit(solution)/shard_map/pallas_call | solution.py:104
  85.9 7.8 %collective-permute-done.12.refs_8_.got_t = bf16[2,384,1024]{2,1,0:T(8,128)(2,1)S(1)} collective-permute-done((bf16[2,384,1024]{2,1,0:T(8,128)(2,1)S(1)}, bf16[2,384,1024]{2,1,0:T(8,128)(2,1)S(1)}, u32[]{:S(2)}, u32[]{:S(2)}) %collective-permute-start.12) | collective-permute-done | bytes 1572896 | tf_op jit(solution)/shard_map/ppermute | solution.py:240
  94.9 6.0 %shard_map.82 = (f32[3,384,512]{2,1,0:T(8,128)}, bf16[3,384,512]{2,1,0:T(8,128)(2,1)}) custom-call(bf16[192,2048]{1,0:T(8,128)(2,1)S(1)} %shard_map.78.refs_0_, bf16[192,2048]{1,0:T(8,128)(2,1)S(1)} %collective-permute-done.7.refs_1_, bf16[2048,1792]{1,0:T(8,128)(2,1)} %refs_2_.13, bf16[2048,1792]{1,0:T(8,128)(2,1)} %refs_3_.9, ...), custom_call_target="tpu_custom_call" | custom-call | flops 1024 | bytes 1024 | tf_op jit(solution)/shard_map/pallas_call | solution.py:104
  101.1 9.5 %collective-permute-done.13.refs_8_.got_g = bf16[1,384,1024]{2,1,0:T(8,128)(2,1)S(1)} collective-permute-done((bf16[1,384,1024]{2,1,0:T(8,128)(2,1)S(1)}, bf16[1,384,1024]{2,1,0:T(8,128)(2,1)S(1)}, u32[]{:S(2)}, u32[]{:S(2)}) %collective-permute-start.13) | collective-permute-done | bytes 786464 | tf_op jit(solution)/shard_map/ppermute | solution.py:240
  110.6 4.2 %shard_map.83 = (f32[3,384,256]{2,1,0:T(8,128)S(1)}, bf16[3,384,256]{2,1,0:T(8,128)(2,1)}) custom-call(bf16[192,2048]{1,0:T(8,128)(2,1)S(1)} %shard_map.78.refs_0_, bf16[192,2048]{1,0:T(8,128)(2,1)S(1)} %collective-permute-done.7.refs_1_, bf16[2048,1792]{1,0:T(8,128)(2,1)} %refs_2_.13, bf16[2048,1792]{1,0:T(8,128)(2,1)} %refs_3_.9, ...), custom_call_target="tpu_custom_call" | custom-call | flops 1024 | bytes 1024 | tf_op jit(solution)/shard_map/pallas_call | solution.py:104
  115.1 2.4 %shard_map.84 = (bf16[512,2048]{1,0:T(8,128)(2,1)}, bf16[2048,512]{1,0:T(8,128)(2,1)}) custom-call(bf16[192,2048]{1,0:T(8,128)(2,1)S(1)} %shard_map.78.refs_0_, bf16[192,2048]{1,0:T(8,128)(2,1)S(1)} %collective-permute-done.7.refs_1_, bf16[64,2048]{1,0:T(8,128)(2,1)S(1)} %copy-done.10, bf16[64,2048]{1,0:T(8,128)(2,1)S(1)} %copy-done.14, ...), custom_call_target="tpu_custom_call" | custom-call | flops 1024 | bytes 1024 | tf_op jit(solution)/shard_map/pallas_call | solution.py:135
  119.4 8.0 %shard_map.86 = (bf16[2048,1792]{1,0:T(8,128)(2,1)}, bf16[2048,1792]{1,0:T(8,128)(2,1)}, bf16[1792,2048]{1,0:T(8,128)(2,1)}) custom-call(f32[3,128,512]{2,1,0:T(8,128)S(1)} %get-tuple-element.25.refs_7_.own_a, bf16[3,128,512]{2,1,0:T(8,128)(2,1)S(1)} %copy-done.16, f32[2,384,1024]{2,1,0:T(8,128)} %get-tuple-element.29.refs_3_.refs_4_.own_t, ...), custom_call_target="tpu_custom_call" | custom-call | flops 1024 | bytes 1024 | tf_op jit(solution)/shard_map/pallas_call | solution.py:211
  127.4 8.1 %shard_map.87 = (bf16[2048,1792]{1,0:T(8,128)(2,1)}, bf16[2048,1792]{1,0:T(8,128)(2,1)}, bf16[1792,2048]{1,0:T(8,128)(2,1)}) custom-call(f32[3,128,1280]{2,1,0:T(8,128)} %copy-done.3, bf16[3,128,1280]{2,1,0:T(8,128)(2,1)S(1)} %collective-permute-done.2.refs_4_.got_a, ...), custom_call_target="tpu_custom_call", output_to_operand_aliasing={{0}: (8, {}), {1}: (9, {}), {2}: (10, {})} | custom-call | flops 1024 | bytes 1024 | tf_op jit(solution)/shard_map/pallas_call | solution.py:211
  136.0 8.1 %shard_map.88 = (bf16[2048,1792]{1,0:T(8,128)(2,1)}, bf16[2048,1792]{1,0:T(8,128)(2,1)}, bf16[1792,2048]{1,0:T(8,128)(2,1)}) custom-call(f32[3,128,1280]{2,1,0:T(8,128)S(1)} %copy-done.4, bf16[3,128,1280]{2,1,0:T(8,128)(2,1)S(1)} %collective-permute-done.2.refs_4_.got_a, ...), custom_call_target="tpu_custom_call", output_to_operand_aliasing={{0}: (8, {}), {1}: (9, {}), {2}: (10, {})} | custom-call | flops 1024 | bytes 1024 | tf_op jit(solution)/shard_map/pallas_call | solution.py:211
  144.1 1.6 %collective-permute-done.14.got_t.got_g = bf16[3,384,256]{2,1,0:T(8,128)(2,1)} collective-permute-done((bf16[3,384,256]{2,1,0:T(8,128)(2,1)}, bf16[3,384,256]{2,1,0:T(8,128)(2,1)}, u32[]{:S(2)}, u32[]{:S(2)}) %collective-permute-start.14) | collective-permute-done | bytes 589856 | tf_op jit(solution)/shard_map/ppermute | solution.py:240
  145.7 5.7 %shard_map.89 = (bf16[2048,1792]{1,0:T(8,128)(2,1)}, bf16[2048,1792]{1,0:T(8,128)(2,1)}, bf16[1792,2048]{1,0:T(8,128)(2,1)}) custom-call(f32[3,128,1280]{2,1,0:T(8,128)S(1)} %copy-done.4, bf16[3,128,1280]{2,1,0:T(8,128)(2,1)S(1)} %collective-permute-done.2.refs_4_.got_a, ...), custom_call_target="tpu_custom_call", output_to_operand_aliasing={{0}: (8, {}), {1}: (9, {}), {2}: (10, {})} | custom-call | flops 1024 | bytes 1024 | tf_op jit(solution)/shard_map/pallas_call | solution.py:211
  (56 shorter events, 13.7 us)
Async XLA Ops:
  0.6 1.9 %collective-permute-start = (bf16[64,2048]{1,0:T(8,128)(2,1)}, bf16[64,2048]{1,0:T(8,128)(2,1)S(1)}, u32[]{:S(2)}, u32[]{:S(2)}) collective-permute-start(bf16[64,2048]{1,0:T(8,128)(2,1)} %refs_2_.14), channel_id=1, source_target_pairs={{0,2},{2,0},{4,6},{6,4},{8,10},{10,8},{12,14},{14,12},{1,3},{3,1},... | collective-permute-start | bytes 786440 | tf_op jit(solution)/shard_map/ppermute | solution.py:243
  1.1 1.7 %collective-permute-start.1 = (bf16[64,2048]{1,0:T(8,128)(2,1)}, bf16[64,2048]{1,0:T(8,128)(2,1)S(1)}, u32[]{:S(2)}, u32[]{:S(2)}) collective-permute-start(bf16[64,2048]{1,0:T(8,128)(2,1)} %refs_2_.15), channel_id=1, source_target_pairs={{0,2},{2,0},{4,6},{6,4},{8,10},{10,8},{12,14},{14,12},{1,3},{3,1},... | collective-permute-start | bytes 786440 | tf_op jit(solution)/shard_map/ppermute | solution.py:243
  2.5 15.3 %copy-start.13 = (bf16[64,2048]{1,0:T(8,128)(2,1)}, bf16[64,2048]{1,0:T(8,128)(2,1)S(1)}, u32[]{:S(2)}) copy-start(bf16[64,2048]{1,0:T(8,128)(2,1)S(1)} %collective-permute-done.refs_1_.refs_3_) | copy-start | bytes 786436
  8.5 24.7 %collective-permute-start.6 = (bf16[3,128,512]{2,1,0:T(8,128)(2,1)S(1)}, bf16[3,128,512]{2,1,0:T(8,128)(2,1)S(1)}, u32[]{:S(2)}, u32[]{:S(2)}) collective-permute-start(bf16[3,128,512]{2,1,0:T(8,128)(2,1)S(1)} %get-tuple-element.28), channel_id=1, source_target_pairs={{0,1},{1,0},{2,3},{3,2},{4,5},{5,4},{6,7},{7,6},{8,9},{9,8},{10,11... | collective-permute-start | bytes 1179656 | tf_op jit(solution)/shard_map/ppermute | solution.py:240
  11.4 21.4 %collective-permute-start.4 = (bf16[64,2048]{1,0:T(8,128)(2,1)S(1)}, bf16[64,2048]{1,0:T(8,128)(2,1)S(1)}, u32[]{:S(2)}, u32[]{:S(2)}) collective-permute-start(bf16[64,2048]{1,0:T(8,128)(2,1)S(1)} %copy-done.9), channel_id=1, source_target_pairs={{0,8},{2,10},{4,12},{6,14},{8,0},{10,2},{12,4},{14,6},{1,9},{3,11}... | collective-permute-start | bytes 786440 | tf_op jit(solution)/shard_map/ppermute | solution.py:247
  14.0 18.8 %collective-permute-start.3 = (bf16[64,2048]{1,0:T(8,128)(2,1)S(1)}, bf16[64,2048]{1,0:T(8,128)(2,1)S(1)}, u32[]{:S(2)}, u32[]{:S(2)}) collective-permute-start(bf16[64,2048]{1,0:T(8,128)(2,1)S(1)} %copy-done.9), channel_id=1, source_target_pairs={{0,4},{2,6},{4,8},{6,10},{8,12},{10,14},{12,0},{14,2},{1,5},{3,7},... | collective-permute-start | bytes 786440 | tf_op jit(solution)/shard_map/ppermute | solution.py:247
  15.6 17.6 %collective-permute-start.5 = (bf16[64,2048]{1,0:T(8,128)(2,1)S(1)}, bf16[64,2048]{1,0:T(8,128)(2,1)S(1)}, u32[]{:S(2)}, u32[]{:S(2)}) collective-permute-start(bf16[64,2048]{1,0:T(8,128)(2,1)S(1)} %copy-done.9), channel_id=1, source_target_pairs={{0,12},{2,14},{4,0},{6,2},{8,4},{10,6},{12,8},{14,10},{1,13},{3,15... | collective-permute-start | bytes 786440 | tf_op jit(solution)/shard_map/ppermute | solution.py:247
  26.1 30.3 %copy-start.3 = (f32[3,128,1280]{2,1,0:T(8,128)}, f32[3,128,1280]{2,1,0:T(8,128)S(1)}, u32[]{:S(2)}) copy-start(f32[3,128,1280]{2,1,0:T(8,128)S(1)} %get-tuple-element.26.refs_3_.own_a) | copy-start | bytes 5898244
  26.1 22.7 %collective-permute-start.2 = (bf16[3,128,1280]{2,1,0:T(8,128)(2,1)S(1)}, bf16[3,128,1280]{2,1,0:T(8,128)(2,1)S(1)}, u32[]{:S(2)}, u32[]{:S(2)}) collective-permute-start(bf16[3,128,1280]{2,1,0:T(8,128)(2,1)S(1)} %get-tuple-element.27), channel_id=1, source_target_pairs={{0,1},{1,0},{2,3},{3,2},{4,5},{5,4},{6,7},{7,6},{8,9},{9,8},{10,11... | collective-permute-start | bytes 2949128 | tf_op jit(solution)/shard_map/ppermute | solution.py:240
  33.2 15.7 %copy-start.15 = (bf16[3,128,512]{2,1,0:T(8,128)(2,1)}, bf16[3,128,512]{2,1,0:T(8,128)(2,1)S(1)}, u32[]{:S(2)}) copy-start(bf16[3,128,512]{2,1,0:T(8,128)(2,1)S(1)} %collective-permute-done.6.refs_4_.got_a) | copy-start | bytes 1179652
  33.5 15.4 %collective-permute-start.7 = (bf16[192,2048]{1,0:T(8,128)(2,1)S(1)}, bf16[192,2048]{1,0:T(8,128)(2,1)S(1)}, u32[]{:S(2)}, u32[]{:S(2)}) collective-permute-start(bf16[192,2048]{1,0:T(8,128)(2,1)S(1)} %shard_map.78.refs_0_), channel_id=1, source_target_pairs={{0,2},{2,0},{4,6},{6,4},{8,10},{10,8},{12,14},{14,12},{1,3},{3,1},... | collective-permute-start | bytes 2359304 | tf_op jit(solution)/shard_map/ppermute | solution.py:243
  56.4 37.3 %collective-permute-start.12 = (bf16[2,384,1024]{2,1,0:T(8,128)(2,1)S(1)}, bf16[2,384,1024]{2,1,0:T(8,128)(2,1)S(1)}, u32[]{:S(2)}, u32[]{:S(2)}) collective-permute-start(bf16[2,384,1024]{2,1,0:T(8,128)(2,1)S(1)} %get-tuple-element.31), channel_id=1, source_target_pairs={{0,1},{1,0},{2,3},{3,2},{4,5},{5,4},{6,7},{7,6},{8,9},{9,8},{10,11... | collective-permute-start | bytes 4718600 | tf_op jit(solution)/shard_map/ppermute | solution.py:240
  56.9 17.5 %collective-permute-start.9 = (bf16[64,2048]{1,0:T(8,128)(2,1)S(1)}, bf16[64,2048]{1,0:T(8,128)(2,1)S(1)}, u32[]{:S(2)}, u32[]{:S(2)}) collective-permute-start(bf16[64,2048]{1,0:T(8,128)(2,1)S(1)} %copy-done.11), channel_id=1, source_target_pairs={{0,8},{2,10},{4,12},{6,14},{8,0},{10,2},{12,4},{14,6},{1,9},{3,11}... | collective-permute-start | bytes 786440 | tf_op jit(solution)/shard_map/ppermute | solution.py:247
  57.0 17.5 %collective-permute-start.8 = (bf16[64,2048]{1,0:T(8,128)(2,1)S(1)}, bf16[64,2048]{1,0:T(8,128)(2,1)S(1)}, u32[]{:S(2)}, u32[]{:S(2)}) collective-permute-start(bf16[64,2048]{1,0:T(8,128)(2,1)S(1)} %copy-done.11), channel_id=1, source_target_pairs={{0,4},{2,6},{4,8},{6,10},{8,12},{10,14},{12,0},{14,2},{1,5},{3,7},... | collective-permute-start | bytes 786440 | tf_op jit(solution)/shard_map/ppermute | solution.py:247
  57.8 17.6 %collective-permute-start.10 = (bf16[64,2048]{1,0:T(8,128)(2,1)S(1)}, bf16[64,2048]{1,0:T(8,128)(2,1)S(1)}, u32[]{:S(2)}, u32[]{:S(2)}) collective-permute-start(bf16[64,2048]{1,0:T(8,128)(2,1)S(1)} %copy-done.11), channel_id=1, source_target_pairs={{0,12},{2,14},{4,0},{6,2},{8,4},{10,6},{12,8},{14,10},{1,13},{3,15... | collective-permute-start | bytes 786440 | tf_op jit(solution)/shard_map/ppermute | solution.py:247
  77.5 2.4 %collective-permute-start.11 = (bf16[192,2048]{1,0:T(8,128)(2,1)S(1)}, bf16[192,2048]{1,0:T(8,128)(2,1)S(1)}, u32[]{:S(2)}, u32[]{:S(2)}) collective-permute-start(bf16[192,2048]{1,0:T(8,128)(2,1)S(1)} %shard_map.80.refs_0_.refs_4_), channel_id=1, source_target_pairs={{0,2},{2,0},{4,6},{6,4},{8,10},{10,8},{12,14},{14,12},{1,3},{3,1},... | collective-permute-start | bytes 2359304 | tf_op jit(solution)/shard_map/ppermute | solution.py:243
  84.3 33.1 %copy-start.5 = (f32[1,384,1024]{2,1,0:T(8,128)}, f32[1,384,1024]{2,1,0:T(8,128)S(1)}, u32[]{:S(2)}) copy-start(f32[1,384,1024]{2,1,0:T(8,128)S(1)} %get-tuple-element.30.refs_7_.refs_4_.own_g) | copy-start | bytes 4718596
  84.3 26.3 %collective-permute-start.13 = (bf16[1,384,1024]{2,1,0:T(8,128)(2,1)S(1)}, bf16[1,384,1024]{2,1,0:T(8,128)(2,1)S(1)}, u32[]{:S(2)}, u32[]{:S(2)}) collective-permute-start(bf16[1,384,1024]{2,1,0:T(8,128)(2,1)S(1)} %get-tuple-element.33), channel_id=1, source_target_pairs={{0,1},{1,0},{2,3},{3,2},{4,5},{5,4},{6,7},{7,6},{8,9},{9,8},{10,11... | collective-permute-start | bytes 2359304 | tf_op jit(solution)/shard_map/ppermute | solution.py:240
  100.9 35.1 %collective-permute-start.15 = (bf16[3,384,512]{2,1,0:T(8,128)(2,1)}, bf16[3,384,512]{2,1,0:T(8,128)(2,1)}, u32[]{:S(2)}, u32[]{:S(2)}) collective-permute-start(bf16[3,384,512]{2,1,0:T(8,128)(2,1)} %get-tuple-element.37), channel_id=1, source_target_pairs={{0,1},{1,0},{2,3},{3,2},{4,5},{5,4},{6,7},{7,6},{8,9},{9,8},{10,11... | collective-permute-start | bytes 3538952 | tf_op jit(solution)/shard_map/ppermute | solution.py:240
  110.6 6.9 %copy-start.12 = (bf16[64,2048]{1,0:T(8,128)(2,1)S(1)}, bf16[64,2048]{1,0:T(8,128)(2,1)}, u32[]{:S(2)}) copy-start(bf16[64,2048]{1,0:T(8,128)(2,1)} %refs_2_.15) | copy-start | bytes 786436
  114.8 30.9 %collective-permute-start.14 = (bf16[3,384,256]{2,1,0:T(8,128)(2,1)}, bf16[3,384,256]{2,1,0:T(8,128)(2,1)}, u32[]{:S(2)}, u32[]{:S(2)}) collective-permute-start(bf16[3,384,256]{2,1,0:T(8,128)(2,1)} %get-tuple-element.35), channel_id=1, source_target_pairs={{0,1},{1,0},{2,3},{3,2},{4,5},{5,4},{6,7},{7,6},{8,9},{9,8},{10,11... | collective-permute-start | bytes 1769480 | tf_op jit(solution)/shard_map/ppermute | solution.py:240
  119.3 8.0 %copy-start.6 = (f32[1,384,1024]{2,1,0:T(8,128)S(1)}, f32[1,384,1024]{2,1,0:T(8,128)}, u32[]{:S(2)}) copy-start(f32[1,384,1024]{2,1,0:T(8,128)} %copy-done.5) | copy-start | bytes 4718596
  127.4 8.6 %copy-start.2 = (bf16[2048,512]{1,0:T(8,128)(2,1)S(1)}, bf16[2048,512]{1,0:T(8,128)(2,1)}, u32[]{:S(2)}) copy-start(bf16[2048,512]{1,0:T(8,128)(2,1)} %get-tuple-element.36.flipped) | copy-start | bytes 6291460
  127.4 8.6 %copy-start.4 = (f32[3,128,1280]{2,1,0:T(8,128)S(1)}, f32[3,128,1280]{2,1,0:T(8,128)}, u32[]{:S(2)}) copy-start(f32[3,128,1280]{2,1,0:T(8,128)} %copy-done.3) | copy-start | bytes 5898244
  (9 other events, 24.4 us)
